TPU v7x, 512 devices: a whole 4x4x16 slice. The times are simulated.
512 devices in a mesh: gx: 4 (over x), gy: 4 (over y), gz: 32 (over z, core).
Axes of the slice: x: 4, y: 4, z: 16, core: 2. Of those that a mesh axis runs over, the one named last changes fastest.
Arguments:
- velocity: float32 [3, 16, 16, 256, 512], P(None, 'gx', 'gy', 'gz'), may hold values from -6 to 6
- viscosity: float32 [16, 16, 256, 512], P('gx', 'gy', 'gz'), may hold values from 0.1 to 1
- fibre_coords: float32 [4, 4, 32, 32, 4, 3, 128], P('gx', 'gy', 'gz'), may hold values from -1 to 1
- fibre_elem: int32 [4, 4, 32, 32, 4], P('gx', 'gy', 'gz'), may hold values from 0 to 127
- block_count: int32 [4, 4, 32, 32], P('gx', 'gy', 'gz'), may hold values from 0 to 4, as said below
- fibre_velocity: float32 [4, 4, 32, 32, 4, 3, 128], P('gx', 'gy', 'gz'), may hold values from -6 to 6
Outputs:
- advection: float32 [3, 16, 16, 256, 512], P(None, 'gx', 'gy', 'gz')
- helmholtz: float32 [3, 16, 16, 256, 512], P(None, 'gx', 'gy', 'gz')
- fibre_drag: float32 [4, 4, 32, 32, 4, 3, 128], P('gx', 'gy', 'gz')
Inputs may be any that keep to these rules, and one draw needn't show every extreme that they name: `fibre_elem`: local element index a * 4 * 8 + b * 8 + c on the destination device. The first block_count of the 4 slots to a destination are live; each device has a destination with all 4 slots live.
All inputs are finite; a program needn't handle non-finite values.
Results may differ from a plain program's by a relative error of at most 0.0003.
Values sent between devices are 32-bit elements; how exact they have to be, the bound alone decides.
No kernel may reach another device: no remote copies, remote signals or barrier semaphores. Data moves between devices by JAX's collectives and lax.ppermute only.
A program may use at most 128 MiB of HBM per device.

v0:
```python
import jax
import jax.numpy as jnp
import numpy as np
from jax import lax
from jax.sharding import PartitionSpec as P

gll_points = (
    -1.0,
    -0.8717401485096066,
    -0.5917001814331423,
    -0.2092992179024789,
    0.2092992179024789,
    0.5917001814331423,
    0.8717401485096066,
    1.0,
)
gll_weights = (
    0.03571428571428571,
    0.2107042271435061,
    0.3411226924835044,
    0.4124587946587038,
    0.4124587946587038,
    0.3411226924835044,
    0.2107042271435061,
    0.03571428571428571,
)
helm_shift = 20.0
drag_scale = 0.5
highest = lax.Precision.HIGHEST


def padded(x, sides, width):
    for axis, dim in sides:
        size, length = (lax.axis_size(axis), x.shape[dim])
        up = [(i, (i + 1) % size) for i in range(size - 1)]
        down = [(j, i) for i, j in up]
        last = lax.slice_in_dim(x, length - width, length, axis=dim)
        first = lax.slice_in_dim(x, 0, width, axis=dim)
        before = lax.ppermute(last, axis, up)
        after = lax.ppermute(first, axis, down)
        x = jnp.concatenate([before, x, after], axis=dim)
    return x


def derivative_table():
    points = list(gll_points)
    barycentric = [1.0] * 8
    for row in range(8):
        for other in range(8):
            if other != row:
                barycentric[row] = barycentric[row] / (points[row] - points[other])
    derivative = np.zeros((8, 8))
    for row in range(8):
        total = 0.0
        for other in range(8):
            if other != row:
                entry = barycentric[other] / barycentric[row] / (points[row] - points[other])
                derivative[row, other] = entry
                total = total + entry
        derivative[row, row] = -total
    return derivative


def operator_tables():
    derivative = derivative_table()
    identity = np.eye(8)
    kron_x = np.kron(np.kron(derivative, identity), identity)
    kron_y = np.kron(np.kron(identity, derivative), identity)
    kron_z = np.kron(np.kron(identity, identity), derivative)
    forward_all = np.concatenate([kron_x.T, kron_y.T, kron_z.T], 1)
    backward_all = np.concatenate([kron_x, kron_y, kron_z], 0)
    weights = np.asarray(gll_weights)
    mass_table = (weights[:, None, None] * weights[None, :, None] * weights[None, None, :]).reshape(
        512
    )
    return (
        jnp.asarray(forward_all, jnp.float32),
        jnp.asarray(backward_all, jnp.float32),
        jnp.asarray(mass_table, jnp.float32),
    )


def face_tables(direction):
    extract = np.zeros((512, 128))
    take_lower = np.zeros((128, 512))
    take_upper = np.zeros((128, 512))
    for node in range(512):
        place = (node // 64, node // 8 % 8, node % 8)
        others = [place[axis_index] for axis_index in range(3) if axis_index != direction]
        column = others[0] * 8 + others[1]
        if place[direction] == 0:
            extract[node, column] = 1.0
            take_lower[64 + column, node] = 1.0
        if place[direction] == 7:
            extract[node, 64 + column] = 1.0
            take_upper[column, node] = 1.0
    return (
        jnp.asarray(extract, jnp.float32),
        jnp.asarray(take_lower, jnp.float32),
        jnp.asarray(take_upper, jnp.float32),
    )


def fluid_terms(velocity, viscosity):
    forward_all, backward_all, mass_table = operator_tables()
    gradient = jnp.dot(velocity, forward_all, precision=highest)
    advected = velocity[0] * gradient[..., 0:512]
    advected = advected + velocity[1] * gradient[..., 512:1024]
    advected = advected + velocity[2] * gradient[..., 1024:1536]
    convective = mass_table * advected
    weighted = mass_table * viscosity
    weighted_all = jnp.concatenate([weighted, weighted, weighted], -1)
    stiffness = jnp.dot(weighted_all * gradient, backward_all, precision=highest)
    helmholtz = stiffness + helm_shift * mass_table * velocity
    return jnp.concatenate([convective, helmholtz], 0)


def face_values(field, direction):
    extract, take_lower, take_upper = face_tables(direction)
    return jnp.dot(field, extract, precision=highest)


def add_neighbours(field, padded_faces, direction):
    extract, take_lower, take_upper = face_tables(direction)
    axis_index = direction + 1
    length = padded_faces.shape[axis_index]
    before = lax.slice_in_dim(padded_faces, 0, length - 2, 1, axis_index)
    after = lax.slice_in_dim(padded_faces, 2, length, 1, axis_index)
    field = field + jnp.dot(before, take_lower, precision=highest)
    return field + jnp.dot(after, take_upper, precision=highest)


def lagrange_rows(position):
    rows = []
    for node in range(8):
        value = jnp.ones_like(position)
        for other in range(8):
            if other != node:
                value = value * (
                    (position - gll_points[other]) / (gll_points[node] - gll_points[other])
                )
        rows.append(value)
    return jnp.stack(rows, -2)


def interpolate(blocks, coords):
    basis_x = lagrange_rows(coords[..., 0, :])
    basis_y = lagrange_rows(coords[..., 1, :])
    basis_z = lagrange_rows(coords[..., 2, :])
    leading = basis_x.shape[:-2]
    width = basis_x.shape[-1]
    weights = (
        basis_x[..., :, None, None, :]
        * basis_y[..., None, :, None, :]
        * basis_z[..., None, None, :, :]
    )
    weights = weights.reshape(leading + (512, width))
    return jnp.einsum("...cn,...np->...cp", blocks, weights, precision=highest)


def drag_of(sampled, own_velocity, counts):
    relative = sampled - own_velocity
    speed_factor = jnp.sqrt(1.0 + jnp.sum(relative * relative, axis=-2, keepdims=True))
    slot_index = lax.broadcasted_iota(jnp.int32, relative.shape[:2], 1)
    live_mask = (slot_index < counts[:, None])[:, :, None, None]
    return jnp.where(live_mask, drag_scale * speed_factor * relative, jnp.zeros_like(relative))


def body(velocity, viscosity, fibre_coords, fibre_elem, block_count, fibre_velocity):
    local_terms = fluid_terms(velocity, viscosity)
    assembled = local_terms
    faces = face_values(assembled, 0)
    assembled = add_neighbours(assembled, padded(faces, (("gx", 1),), 1), 0)
    faces = face_values(assembled, 1)
    assembled = add_neighbours(assembled, padded(faces, (("gy", 2),), 1), 1)
    faces = face_values(assembled, 2)
    assembled = add_neighbours(assembled, padded(faces, (("gz", 3),), 1), 2)
    coords = fibre_coords.reshape(fibre_coords.shape[3:])
    idents = fibre_elem.reshape(fibre_elem.shape[3:])
    counts = block_count.reshape(block_count.shape[3:])
    own_velocity = fibre_velocity.reshape(fibre_velocity.shape[3:])
    element_table = jnp.moveaxis(velocity.reshape(3, -1, velocity.shape[-1]), 1, 0)
    got_coords = lax.all_to_all(coords, "gz", split_axis=0, concat_axis=0, tiled=True)
    got_idents = lax.all_to_all(idents, "gz", split_axis=0, concat_axis=0, tiled=True)
    values = interpolate(element_table[got_idents], got_coords)
    sampled = lax.all_to_all(values, "gz", split_axis=0, concat_axis=0, tiled=True)
    fibre_drag = drag_of(sampled, own_velocity, counts)
    return (assembled[:3], assembled[3:], fibre_drag.reshape(fibre_coords.shape))


def solution(mesh):
    in_specs = (
        P(None, "gx", "gy", "gz", None),
        P("gx", "gy", "gz", None),
        P("gx", "gy", "gz", None, None, None, None),
        P("gx", "gy", "gz", None, None),
        P("gx", "gy", "gz", None),
        P("gx", "gy", "gz", None, None, None, None),
    )
    out_specs = (
        P(None, "gx", "gy", "gz", None),
        P(None, "gx", "gy", "gz", None),
        P("gx", "gy", "gz", None, None, None, None),
    )
    return jax.shard_map(body, mesh=mesh, in_specs=in_specs, out_specs=out_specs, check_vma=False)
```

profile of v0, /device:TPU:6, one launch (start us, length us, event | category | flops | bytes accessed | tf_op | source)
XLA Modules:
  0.0 151.9 jit_solution(11888300097690547614)
XLA Ops:
  0.6 1.4 copy.65
  2.1 15.5 %all-to-all-start = ((s32[32,1,4]{2,1,0:T(1,128)}), s32[32,1,4]{2,1,0:T(1,128)S(1)}, u32[]{:S(2)}, u32[]{:S(2)}) async-start(s32[32,1,4]{2,1,0:T(1,128)} %copy.65), calls=%async_computation | async-start | bytes 32768 | tf_op jit(solution)/shard_map/all_to_all | solution.py:184
  17.6 1.2 slice_bitcast_fusion.2
  18.8 6.0 %convolution_bitcast_fusion = f32[3,4,4,8,1536]{4,3,2,1,0:T(8,128)S(1)} fusion(f32[512,1536,1,1,1]{1,0,4,3,2:T(8,128)} %constant.326, f32[3,4,4,8,512]{4,3,2,1,0:T(8,128)S(1)} %copy-done), kind=kOutput, calls=%fused_computation.2 | convolution fusion | flops 3623878656 | bytes 6291456 | tf_op jit(solution)/shard_map/dot_general | solution.py:106
  24.8 0.1 pad_maximum_fusion.2
  24.9 0.4 fusion.8
  25.3 1.5 copy-done.5
  26.8 4.1 %fusion.2 = f32[3,4,4,8,512]{4,3,2,1,0:T(8,128)S(1)} fusion(f32[1536,512,1,1,1]{1,0,4,3,2:T(8,128)S(1)} %copy-done.5, f32[3,4,4,8,1536]{4,3,2,1,0:T(8,128)S(1)} %convolution_bitcast_fusion, f32[4,4,8,1536]{3,2,1,0:T(8,128)S(1)} %pad_maximum_fusion.2, f32[3,4,4,8,512]{4,3,2,1,0:T(8,128)S(1)} %copy-done, f32[512]{0:T(512)S(1)} %copy-done.16), kind=kOutput, calls=%fused_computation.10 | convolution fusion | flops 3624861696 | bytes 7866368 | tf_op jit(solution)/shard_map/dot_general | solution.py:113
  30.9 0.9 copy-done.1
  31.8 1.4 fusion.5
  33.2 1.4 collective-permute-start
  34.7 5.2 %collective-permute-start.1 = (f32[6,1,4,8,128]{4,3,2,1,0:T(8,128)S(1)}, f32[6,1,4,8,128]{4,3,2,1,0:T(8,128)}, u32[]{:S(2)}, u32[]{:S(2)}) collective-permute-start(f32[6,1,4,8,128]{4,3,2,1,0:T(8,128)S(1)} %get-tuple-element.18), channel_id=1, source_target_pairs={{128,0},{256,128},{384,256},{129,1},{257,129},{385,257},{130,2},{2... | collective-permute-start | bytes 294920 | tf_op jit(solution)/shard_map/ppermute | solution.py:40
  39.8 0.1 iota_compare_fusion
  39.9 1.5 %copy.64 = f32[3,4,4,8,512]{4,0,3,2,1:T(4,128)} copy(f32[3,4,4,8,512]{4,3,2,1,0:T(8,128)S(1)} %copy-done) | data formatting | bytes 1572864 | tf_op args[0]
  41.4 12.6 %all-to-all-start.1 = ((f32[32,4,3,128]{3,1,2,0:T(4,128)}), f32[32,4,3,128]{3,1,2,0:T(4,128)}, u32[]{:S(2)}, u32[]{:S(2)}) async-start(f32[32,4,3,128]{3,1,2,0:T(4,128)} %bitcast.32), calls=%async_computation.1 | async-start | bytes 393216 | tf_op jit(solution)/shard_map/all_to_all | solution.py:183
  54.1 0.1 copy.66
  54.1 0.1 copy.67
  54.2 0.1 reshape.103
  54.4 1.4 fusion.10
  55.8 2.6 %add_add_fusion.2 = f32[6,4,4,8,512]{4,3,2,1,0:T(8,128)S(1)} fusion(f32[6,4,4,8,512]{4,3,2,1,0:T(8,128)S(1)} %fusion.10, f32[3,4,4,8,512]{4,3,2,1,0:T(8,128)S(1)} %copy-done.2, f32[3,4,4,8,512]{4,3,2,1,0:T(8,128)S(1)} %fusion.8, f32[128,512,1,1,1]{1,0,4,3,2:T(8,128)} %constant.330, f32[6,1,4,8,128]{4,3,2,1,0:T(8,128)} %collective-permute-done.1, ...), kind=kOutput, calls=%fused_computation.9 | convolution fusion | flops 605282304 | bytes 5472256 | tf_op jit(solution)/shard_map/dot_general | solution.py:130
  58.4 1.4 fusion.46
  59.8 0.7 fusion.43
  60.5 3.5 %collective-permute-start.2 = (f32[6,4,1,8,128]{4,3,2,1,0:T(8,128)}, f32[6,4,1,8,128]{4,3,2,1,0:T(8,128)S(1)}, u32[]{:S(2)}, u32[]{:S(2)}) collective-permute-start(f32[6,4,1,8,128]{4,3,2,1,0:T(8,128)} %get-tuple-element.17), channel_id=1, source_target_pairs={{0,32},{32,64},{64,96},{1,33},{33,65},{65,97},{2,34},{34,66},{66,9... | collective-permute-start | bytes 294920 | tf_op jit(solution)/shard_map/ppermute | solution.py:39
  64.0 2.1 %gather_fusion = f32[128,3,512]{2,1,0:T(4,128)} fusion(f32[128,3,512]{2,1,0:T(4,128)S(1)} %bitcast.79, s32[1024]{0:T(1024)S(1)} %pad_clamp_fusion), kind=kCustom, calls=%fused_computation | custom fusion | bytes 1573376 | tf_op jit(solution)/shard_map/gather | solution.py:185
  66.1 1.4 collective-permute-start.3
  67.5 1.4 fusion.20
  68.9 3.8 %collective-permute-done.3 = f32[6,4,1,8,128]{4,3,2,1,0:T(8,128)S(1)} collective-permute-done((f32[6,4,1,8,128]{4,3,2,1,0:T(8,128)S(1)}, f32[6,4,1,8,128]{4,3,2,1,0:T(8,128)S(1)}, u32[]{:S(2)}, u32[]{:S(2)}) %collective-permute-start.3) | collective-permute-done | bytes 98336 | tf_op jit(solution)/shard_map/ppermute | solution.py:40
  72.7 1.5 add_add_fusion.1
  74.2 1.4 fusion.47
  75.6 0.1 fusion.42
  75.6 1.3 collective-permute-start.4
  76.9 1.5 collective-permute-start.5
  78.5 0.9 fusion.45
  80.2 0.1 multiply_dynamic-update-slice_fusion
  80.3 0.3 copy.71
  81.1 0.3 copy.69
  81.4 0.3 copy.73
  81.7 0.8 broadcast_multiply_fusion.1
  82.5 11.5 %broadcast_multiply_fusion = f32[32,4,8,8,8,128]{5,4,3,2,1,0:T(8,128)} fusion(f32[32,4,8,128]{3,2,1,0:T(8,128)S(1)} %copy.73, f32[32,4,8,8,128]{4,3,2,1,0:T(8,128)S(1)} %broadcast_multiply_fusion.1), kind=kLoop, calls=%fused_computation.1 | loop fusion | flops 8388608 | bytes 38273024 | tf_op jit(solution)/shard_map/mul | solution.py:153
  94.0 20.0 %fusion.48 = f32[32,4,3,128]{3,2,1,0:T(4,128)S(1)} fusion(f32[32,4,3,512]{3,2,1,0:T(4,128)S(1)} %bitcast.78, f32[32,4,512,128]{3,2,1,0:T(8,128)} %bitcast.77), kind=kOutput, calls=%fused_computation.91 | convolution fusion | flops 301989888 | bytes 34537472 | tf_op jit(solution)/shard_map/...cn,...np->...cp/dot_general | solution.py:158
  114.1 0.7 copy.74
  114.8 16.1 %all-to-all-start.2 = ((f32[32,4,3,128]{3,1,2,0:T(4,128)}), f32[32,4,3,128]{3,1,2,0:T(4,128)S(1)}, u32[]{:S(2)}, u32[]{:S(2)}) async-start(f32[32,4,3,128]{3,1,2,0:T(4,128)} %copy.74), calls=%async_computation.2 | async-start | bytes 393216 | tf_op jit(solution)/shard_map/all_to_all | solution.py:186
  130.9 1.4 fusion.32
  132.4 1.5 add_add_fusion
  133.8 1.3 fusion.41
  135.1 15.8 %all-to-all-done.2 = f32[32,4,3,128]{3,1,2,0:T(4,128)S(1)} async-done(((f32[32,4,3,128]{3,1,2,0:T(4,128)}), f32[32,4,3,128]{3,1,2,0:T(4,128)S(1)}, u32[]{:S(2)}, u32[]{:S(2)}) %all-to-all-start.2) | async-done | bytes 196640 | tf_op jit(solution)/shard_map/all_to_all | solution.py:186
  151.0 0.1 multiply_reduce_fusion
  151.1 0.8 select_bitcast_fusion
  (70 shorter events, 1.4 us)
Async XLA Ops:
  0.6 18.1 %copy-start = (f32[3,4,4,8,512]{4,3,2,1,0:T(8,128)S(1)}, f32[3,4,4,8,512]{4,3,2,1,0:T(8,128)}, u32[]{:S(2)}) copy-start(f32[3,4,4,8,512]{4,3,2,1,0:T(8,128)} %param.18) | copy-start | bytes 2359300
  2.1 39.4 %all-to-all-start = ((s32[32,1,4]{2,1,0:T(1,128)}), s32[32,1,4]{2,1,0:T(1,128)S(1)}, u32[]{:S(2)}, u32[]{:S(2)}) async-start(s32[32,1,4]{2,1,0:T(1,128)} %copy.65), calls=%async_computation | async-start | bytes 32768 | tf_op jit(solution)/shard_map/all_to_all | solution.py:184
  18.7 6.0 %copy-start.13 = (f32[4,4,8,512]{3,2,1,0:T(8,128)S(1)}, f32[4,4,8,512]{3,2,1,0:T(8,128)}, u32[]{:S(2)}) copy-start(f32[4,4,8,512]{3,2,1,0:T(8,128)} %param.19) | copy-start | bytes 786436
  18.8 6.0 %copy-start.17 = (f32[512]{0:T(512)S(1)}, f32[512]{0:T(512)}, u32[]{:S(2)}) copy-start(f32[512]{0:T(512)} %constant.309.clone) | copy-start | bytes 6148
  24.9 1.9 %copy-start.5 = (f32[1536,512,1,1,1]{1,0,4,3,2:T(8,128)S(1)}, f32[1536,512,1,1,1]{1,0,4,3,2:T(8,128)}, u32[]{:S(2)}) copy-start(f32[1536,512,1,1,1]{1,0,4,3,2:T(8,128)} %constant.327) | copy-start | bytes 9437188
  24.9 1.9 %copy-start.16 = (f32[512]{0:T(512)S(1)}, f32[512]{0:T(512)}, u32[]{:S(2)}) copy-start(f32[512]{0:T(512)} %constant.325) | copy-start | bytes 6148
  26.8 5.0 %copy-start.12 = (f32[512,128,1,1,1]{1,0,4,3,2:T(8,128)S(1)}, f32[512,128,1,1,1]{1,0,4,3,2:T(8,128)}, u32[]{:S(2)}) copy-start(f32[512,128,1,1,1]{1,0,4,3,2:T(8,128)} %constant.328) | copy-start | bytes 786436
  30.9 0.9 copy-start.1
  31.8 8.0 %copy-start.18 = (s32[1,1,1,32]{3,2,1,0:T(1,128)S(1)}, s32[1,1,1,32]{3,2,1,0:T(1,128)}, u32[]{:S(2)}) copy-start(s32[1,1,1,32]{3,2,1,0:T(1,128)} %param.22) | copy-start | bytes 388
  33.2 21.2 %copy-start.11 = (f32[128,512,1,1,1]{1,0,4,3,2:T(8,128)S(1)}, f32[128,512,1,1,1]{1,0,4,3,2:T(8,128)}, u32[]{:S(2)}) copy-start(f32[128,512,1,1,1]{1,0,4,3,2:T(8,128)} %constant.329) | copy-start | bytes 786436
  33.2 21.1 %collective-permute-start = (f32[6,1,4,8,128]{4,3,2,1,0:T(8,128)S(1)}, f32[6,1,4,8,128]{4,3,2,1,0:T(8,128)S(1)}, u32[]{:S(2)}, u32[]{:S(2)}) collective-permute-start(f32[6,1,4,8,128]{4,3,2,1,0:T(8,128)S(1)} %get-tuple-element.19), channel_id=1, source_target_pairs={{0,128},{128,256},{256,384},{1,129},{129,257},{257,385},{2,130},{1... | collective-permute-start | bytes 294920 | tf_op jit(solution)/shard_map/ppermute | solution.py:39
  34.7 21.1 %collective-permute-start.1 = (f32[6,1,4,8,128]{4,3,2,1,0:T(8,128)S(1)}, f32[6,1,4,8,128]{4,3,2,1,0:T(8,128)}, u32[]{:S(2)}, u32[]{:S(2)}) collective-permute-start(f32[6,1,4,8,128]{4,3,2,1,0:T(8,128)S(1)} %get-tuple-element.18), channel_id=1, source_target_pairs={{128,0},{256,128},{384,256},{129,1},{257,129},{385,257},{130,2},{2... | collective-permute-start | bytes 294920 | tf_op jit(solution)/shard_map/ppermute | solution.py:40
  41.4 14.4 %copy-start.2 = (f32[3,4,4,8,512]{4,3,2,1,0:T(8,128)S(1)}, f32[3,4,4,8,512]{4,3,2,1,0:T(8,128)}, u32[]{:S(2)}) copy-start(f32[3,4,4,8,512]{4,3,2,1,0:T(8,128)} %copy-done.1) | copy-start | bytes 2359300
  41.4 37.0 %all-to-all-start.1 = ((f32[32,4,3,128]{3,1,2,0:T(4,128)}), f32[32,4,3,128]{3,1,2,0:T(4,128)}, u32[]{:S(2)}, u32[]{:S(2)}) async-start(f32[32,4,3,128]{3,1,2,0:T(4,128)} %bitcast.32), calls=%async_computation.1 | async-start | bytes 393216 | tf_op jit(solution)/shard_map/all_to_all | solution.py:183
  55.8 2.6 %copy-start.10 = (f32[512,128,1,1,1]{1,0,4,3,2:T(8,128)S(1)}, f32[512,128,1,1,1]{1,0,4,3,2:T(8,128)}, u32[]{:S(2)}) copy-start(f32[512,128,1,1,1]{1,0,4,3,2:T(8,128)} %constant.331) | copy-start | bytes 786436
  58.4 5.6 %copy-start.4 = (f32[3,4,4,8,512]{4,0,3,2,1:T(4,128)S(1)}, f32[3,4,4,8,512]{4,0,3,2,1:T(4,128)}, u32[]{:S(2)}) copy-start(f32[3,4,4,8,512]{4,0,3,2,1:T(4,128)} %copy.64) | copy-start | bytes 2359300
  59.8 7.7 %copy-start.9 = (f32[128,512,1,1,1]{1,0,4,3,2:T(8,128)S(1)}, f32[128,512,1,1,1]{1,0,4,3,2:T(8,128)}, u32[]{:S(2)}) copy-start(f32[128,512,1,1,1]{1,0,4,3,2:T(8,128)} %constant.332) | copy-start | bytes 786436
  60.5 7.0 %collective-permute-start.2 = (f32[6,4,1,8,128]{4,3,2,1,0:T(8,128)}, f32[6,4,1,8,128]{4,3,2,1,0:T(8,128)S(1)}, u32[]{:S(2)}, u32[]{:S(2)}) collective-permute-start(f32[6,4,1,8,128]{4,3,2,1,0:T(8,128)} %get-tuple-element.17), channel_id=1, source_target_pairs={{0,32},{32,64},{64,96},{1,33},{33,65},{65,97},{2,34},{34,66},{66,9... | collective-permute-start | bytes 294920 | tf_op jit(solution)/shard_map/ppermute | solution.py:39
  66.1 6.6 %copy-start.15 = (f32[128,512,1,1,1]{1,0,4,3,2:T(8,128)S(1)}, f32[128,512,1,1,1]{1,0,4,3,2:T(8,128)}, u32[]{:S(2)}) copy-start(f32[128,512,1,1,1]{1,0,4,3,2:T(8,128)} %constant.333) | copy-start | bytes 786436
  66.1 6.6 %collective-permute-start.3 = (f32[6,4,1,8,128]{4,3,2,1,0:T(8,128)S(1)}, f32[6,4,1,8,128]{4,3,2,1,0:T(8,128)S(1)}, u32[]{:S(2)}, u32[]{:S(2)}) collective-permute-start(f32[6,4,1,8,128]{4,3,2,1,0:T(8,128)S(1)} %get-tuple-element.16), channel_id=1, source_target_pairs={{32,0},{64,32},{96,64},{33,1},{65,33},{97,65},{34,2},{66,34},{98,6... | collective-permute-start | bytes 294920 | tf_op jit(solution)/shard_map/ppermute | solution.py:40
  68.9 5.3 %copy-start.8 = (f32[512,128,1,1,1]{1,0,4,3,2:T(8,128)S(1)}, f32[512,128,1,1,1]{1,0,4,3,2:T(8,128)}, u32[]{:S(2)}) copy-start(f32[512,128,1,1,1]{1,0,4,3,2:T(8,128)} %constant.334) | copy-start | bytes 786436
  75.6 55.3 %collective-permute-start.4 = (f32[6,4,4,1,128]{4,3,2,1,0:T(1,128)S(1)}, f32[6,4,4,1,128]{4,3,2,1,0:T(1,128)S(1)}, u32[]{:S(2)}, u32[]{:S(2)}) collective-permute-start(f32[6,4,4,1,128]{4,3,2,1,0:T(1,128)S(1)} %get-tuple-element.15), channel_id=1, source_target_pairs={{0,1},{1,2},{2,3},{3,4},{4,5},{5,6},{6,7},{7,8},{8,9},{9,10},{10,1... | collective-permute-start | bytes 147464 | tf_op jit(solution)/shard_map/ppermute | solution.py:39
  76.9 55.4 %collective-permute-start.5 = (f32[6,4,4,1,128]{4,3,2,1,0:T(1,128)S(1)}, f32[6,4,4,1,128]{4,3,2,1,0:T(1,128)S(1)}, u32[]{:S(2)}, u32[]{:S(2)}) collective-permute-start(f32[6,4,4,1,128]{4,3,2,1,0:T(1,128)S(1)} %get-tuple-element.14), channel_id=1, source_target_pairs={{1,0},{2,1},{3,2},{4,3},{5,4},{6,5},{7,6},{8,7},{9,8},{10,9},{11,1... | collective-permute-start | bytes 147464 | tf_op jit(solution)/shard_map/ppermute | solution.py:40
  82.5 11.5 %copy-start.3 = (f32[128,3,512]{2,1,0:T(4,128)S(1)}, f32[128,3,512]{2,1,0:T(4,128)}, u32[]{:S(2)}) copy-start(f32[128,3,512]{2,1,0:T(4,128)} %gather_fusion) | copy-start | bytes 2359300
  94.0 36.9 %copy-start.7 = (f32[128,512,1,1,1]{1,0,4,3,2:T(8,128)S(1)}, f32[128,512,1,1,1]{1,0,4,3,2:T(8,128)}, u32[]{:S(2)}) copy-start(f32[128,512,1,1,1]{1,0,4,3,2:T(8,128)} %constant.335) | copy-start | bytes 786436
  114.0 18.3 %copy-start.14 = (f32[128,512,1,1,1]{1,0,4,3,2:T(8,128)S(1)}, f32[128,512,1,1,1]{1,0,4,3,2:T(8,128)}, u32[]{:S(2)}) copy-start(f32[128,512,1,1,1]{1,0,4,3,2:T(8,128)} %constant.336) | copy-start | bytes 786436
  114.8 36.2 %all-to-all-start.2 = ((f32[32,4,3,128]{3,1,2,0:T(4,128)}), f32[32,4,3,128]{3,1,2,0:T(4,128)S(1)}, u32[]{:S(2)}, u32[]{:S(2)}) async-start(f32[32,4,3,128]{3,1,2,0:T(4,128)} %copy.74), calls=%async_computation.2 | async-start | bytes 393216 | tf_op jit(solution)/shard_map/all_to_all | solution.py:186
  133.8 17.1 %copy-start.6 = (f32[1,1,1,32,4,3,128]{6,4,5,3,2,1,0:T(4,128)S(1)}, f32[1,1,1,32,4,3,128]{6,4,5,3,2,1,0:T(4,128)}, u32[]{:S(2)}) copy-start(f32[1,1,1,32,4,3,128]{6,4,5,3,2,1,0:T(4,128)} %param.23) | copy-start | bytes 589828
where the time goes:
time: 152 us
  starting transfers between devices  58.5 us (38%)
  matrix products  43.9 us (29%)
  waiting for transfers between devices  19.6 us (13%)
  other arithmetic  15 us (10%)
  local copies, waits for them, and re-layouts  13.6 us (9%)
    dot_general x1, matrix products, interpolate(): return jnp.einsum('...cn,...np->...cp', blocks, weights, precision=highest)  20 us
    all_to_all x1, starting transfers between devices, body(): lax.all_to_all(values, 'gz', split_axis=0, concat_axis=0, tiled=True)  16.1 us
    all_to_all x1, waiting for transfers between devices, body(): lax.all_to_all(values, 'gz', split_axis=0, concat_axis=0, tiled=True)  15.8 us
    all_to_all x1, starting transfers between devices, body(): lax.all_to_all(idents, 'gz', split_axis=0, concat_axis=0, tiled=True)  15.5 us
    all_to_all x1, starting transfers between devices, body(): lax.all_to_all(coords, 'gz', split_axis=0, concat_axis=0, tiled=True)  12.6 us
    mul x2, other arithmetic, interpolate(): basis_x[..., :, None, None, :] * basis_y[..., None, :, None, :]  12.3 us
    ppermute x3, starting transfers between devices, padded(): after = lax.ppermute(first, axis, down)  8.1 us
    ppermute x3, starting transfers between devices, padded(): before = lax.ppermute(last, axis, up)  6.18 us
  transfers between devices with their start and end apart: 9, of which 2 were waited for; matrix products, arithmetic and copies ran while one was open for 45% of the time, Pallas kernels for 0%

commit v1 on v0

v1 whole, which is shorter than its diff:
```python
import jax
import jax.numpy as jnp
import numpy as np
from jax import lax
from jax.experimental import pallas as pl
from jax.experimental.pallas import tpu as pltpu
from jax.sharding import PartitionSpec as P

gll_points = (
    -1.0,
    -0.8717401485096066,
    -0.5917001814331423,
    -0.2092992179024789,
    0.2092992179024789,
    0.5917001814331423,
    0.8717401485096066,
    1.0,
)
gll_weights = (
    0.03571428571428571,
    0.2107042271435061,
    0.3411226924835044,
    0.4124587946587038,
    0.4124587946587038,
    0.3411226924835044,
    0.2107042271435061,
    0.03571428571428571,
)
helm_shift = 20.0
drag_scale = 0.5
UNROLL = 8
VMEM_LIMIT = 48 * 1024 * 1024
f32 = jnp.float32
bf16 = jnp.bfloat16


def derivative_table():
    points = list(gll_points)
    barycentric = [1.0] * 8
    for row in range(8):
        for other in range(8):
            if other != row:
                barycentric[row] = barycentric[row] / (points[row] - points[other])
    derivative = np.zeros((8, 8))
    for row in range(8):
        total = 0.0
        for other in range(8):
            if other != row:
                entry = barycentric[other] / barycentric[row] / (points[row] - points[other])
                derivative[row, other] = entry
                total = total + entry
        derivative[row, row] = -total
    return derivative


def operator_tables():
    derivative = derivative_table()
    identity = np.eye(8)
    kron_x = np.kron(np.kron(derivative, identity), identity)
    kron_y = np.kron(np.eye(4), np.kron(derivative, identity))
    kron_z = np.kron(np.eye(32), derivative)
    kron_yz = np.concatenate([kron_y, kron_z], 0)
    weights = np.asarray(gll_weights)
    mass = (weights[:, None, None] * weights[None, :, None] * weights[None, None, :]).reshape(1, 512)
    return (
        kron_x.astype(np.float32),
        kron_yz.astype(np.float32),
        mass.astype(np.float32),
    )


def pick_table(face):
    node = lax.broadcasted_iota(jnp.int32, (512, 128), 0)
    lane = lax.broadcasted_iota(jnp.int32, (512, 128), 1)
    i, j, k = node >> 6, (node >> 3) & 7, node & 7
    edge = 7 * (face % 2)
    if face < 2:
        hit = (j == edge) & (lane == i * 8 + k)
    else:
        hit = (k == edge) & (lane == i * 8 + j)
    return jnp.where(hit, 1.0, 0.0).astype(bf16)


def edge_table(side, place):
    source = lax.broadcasted_iota(jnp.int32, (128, 128), 0)
    lane = lax.broadcasted_iota(jnp.int32, (128, 128), 1)
    target = (source & 64) + 56 * place + ((source >> 3) & 7)
    hit = ((source & 7) == 7 * side) & (lane == target)
    return jnp.where(hit, 1.0, 0.0).astype(bf16)


def basis_table():
    table = np.zeros((8, 8, 128))
    for node in range(8):
        others = [other for other in range(8) if other != node]
        scale = 1.0
        for place, other in enumerate(others):
            table[place, node] = gll_points[other]
            scale = scale / (gll_points[node] - gll_points[other])
        table[7, node] = scale
    return table.astype(np.float32)


def split(x):
    high = x.astype(bf16)
    low = (x - high.astype(f32)).astype(bf16)
    return high, low


def mm(a, b, dims=((1,), (0,))):
    return lax.dot_general(a, b, (dims, ((), ())), preferred_element_type=f32)


def dot3(x, table, side):
    high, low = split(x)
    dims = ((1,), (side,))
    return mm(high, table[0], dims) + mm(high, table[1], dims) + mm(low, table[0], dims)


def pick(x, table):
    high, low = split(x)
    return mm(high, table) + mm(low, table)


def spread(x, table):
    high, low = split(x)
    dims = ((1,), (1,))
    return mm(high, table, dims) + mm(low, table, dims)


def lane_iota(shape):
    return lax.broadcasted_iota(jnp.int32, shape, len(shape) - 1)


def fluid_kernel(vel_in, visc_in, dx_in, dyz_in, mass_in, adv_out, helm_out, xl, xr, yl, yr, zl, zr, flux, adv, helm, vel, visc, dx_ref, dyz_ref, mass_ref, sems):
    pairs = ((vel_in, vel), (dx_in, dx_ref), (dyz_in, dyz_ref), (visc_in, visc), (mass_in, mass_ref))
    loads = [pltpu.make_async_copy(a, b, sems.at[n]) for n, (a, b) in enumerate(pairs)]
    for load in loads:
        load.start()
    loads[0].wait()
    loads[1].wait()
    v = vel[...].reshape(384, 512)
    dx = split(dx_ref[...])
    flux[0] = dot3(v, dx, 1)
    loads[2].wait()
    dyz = split(dyz_ref[...])
    for half in range(2):
        lanes = slice(256 * half, 256 * half + 256)
        g = dot3(v[:, lanes], dyz, 1)
        flux[1, :, lanes] = g[:, :256]
        flux[2, :, lanes] = g[:, 256:]
    loads[3].wait()
    loads[4].wait()
    mass = mass_ref[...]
    weighted = mass * visc[...]
    for c in range(3):
        rows = slice(128 * c, 128 * c + 128)
        total = vel[0] * flux[0, rows] + vel[1] * flux[1, rows] + vel[2] * flux[2, rows]
        adv[c] = mass * total
        for d in range(3):
            flux[d, rows] = weighted * flux[d, rows]
    stiff = dot3(flux[0], dx, 0)
    helm[...] = (stiff + (helm_shift * mass) * v).reshape(3, 128, 512)
    for half in range(2):
        lanes = slice(256 * half, 256 * half + 256)
        both = jnp.concatenate([flux[1, :, lanes], flux[2, :, lanes]], axis=1)
        helm[:, :, lanes] = helm[:, :, lanes] + dot3(both, dyz, 0).reshape(3, 128, 256)
    stores = []
    for field, out in ((adv, adv_out), (helm, helm_out)):
        for c in range(3):
            local_sums(field, c)
            stores.append(pltpu.make_async_copy(field.at[c], out.at[c], sems.at[5 + len(stores)]))
            stores[-1].start()
    lane = lane_iota((32, 128))
    for c in range(3):
        xl[c] = jnp.where(lane < 64, adv[c, 0:32, 0:128], pltpu.roll(helm[c, 0:32, 0:128], 64, 1))
        xr[c] = jnp.where(lane < 64, pltpu.roll(adv[c, 96:128, 384:512], 64, 1), helm[c, 96:128, 384:512])
    for out, start, side in ((yl, 0, 0), (yr, 24, 1)):
        faces = []
        for field in (adv, helm):
            rows = field[...].reshape(12, 32, 512)[:, start : start + 8].reshape(96, 512)
            faces.append(pick(rows, pick_table(side)))
        out[...] = (faces[0] + pltpu.roll(faces[1], 64, 1)).reshape(3, 32, 128)
    for out, start, side in ((zl, 0, 2), (zr, 7, 3)):
        faces = []
        for field in (adv, helm):
            rows = field[...].reshape(48, 8, 512)[:, start]
            faces.append(pick(rows, pick_table(side)))
        out[...] = (faces[0] + pltpu.roll(faces[1], 64, 1)).reshape(3, 16, 128)
    for store in stores:
        store.wait()


def local_sums(field, c):
    lane = lane_iota((96, 128))
    upper = field[c, 0:96, 384:512]
    lower = field[c, 32:128, 0:128]
    field[c, 0:96, 384:512] = upper + jnp.where(lane >= 64, pltpu.roll(lower, 64, 1), 0.0)
    field[c, 32:128, 0:128] = lower + jnp.where(lane < 64, pltpu.roll(upper, 64, 1), 0.0)
    for tile in range(4):
        lanes = slice(128 * tile, 128 * tile + 128)
        y = field[c, :, lanes].reshape(4, 32, 128)
        below = y[:, 0:24].reshape(96, 128)
        above = y[:, 8:32].reshape(96, 128)
        j = lane // 8 % 8
        to_below = jnp.where(j == 7, pltpu.roll(above, 56, 1), 0.0).reshape(4, 24, 128)
        to_above = jnp.where(j == 0, pltpu.roll(below, 72, 1), 0.0).reshape(4, 24, 128)
        gap = jnp.zeros((4, 8, 128), f32)
        y = y + jnp.concatenate([to_below, gap], 1) + jnp.concatenate([gap, to_above], 1)
        z = y.reshape(16, 8, 128)
        lane_z = lane_iota((16, 8, 128)) % 8
        level = lax.broadcasted_iota(jnp.int32, (16, 8, 128), 1)
        from_below = pltpu.roll(pltpu.roll(z, 121, 2), 1, 1)
        from_above = pltpu.roll(pltpu.roll(z, 7, 2), 7, 1)
        z = z + jnp.where((lane_z == 0) & (level > 0), from_below, 0.0)
        z = z + jnp.where((lane_z == 7) & (level < 7), from_above, 0.0)
        field[c, :, lanes] = z.reshape(128, 128)


def y_face_kernel(xb, xa, yl_in, yr_in, yl, yr):
    lane = lane_iota((8, 128)) % 64
    for c in range(3):
        yl[c, 0:8] = yl_in[c, 0:8] + jnp.where(lane < 8, xb[c, 0:8], 0.0)
        yr[c, 0:8] = yr_in[c, 0:8] + jnp.where(lane < 8, pltpu.roll(xb[c, 24:32], 72, 1), 0.0)
        yl[c, 8:24] = yl_in[c, 8:24]
        yr[c, 8:24] = yr_in[c, 8:24]
        yl[c, 24:32] = yl_in[c, 24:32] + jnp.where(lane >= 56, pltpu.roll(xa[c, 0:8], 56, 1), 0.0)
        yr[c, 24:32] = yr_in[c, 24:32] + jnp.where(lane >= 56, xa[c, 24:32], 0.0)


def z_face_kernel(xb, xa, yb, ya, zl_in, zr_in, zl, zr):
    zl[...] = zl_in[...]
    zr[...] = zr_in[...]
    lane = lane_iota((1, 128)) % 8
    for out, level, side in ((zl, 0, 0), (zr, 7, 1)):
        for got, place in ((xb, 0), (xa, 1)):
            part = pick(got[...].reshape(96, 128), edge_table(side, place))
            for c in range(3):
                for b in range(4):
                    source = 32 * c + 8 * b + level
                    row = 12 * place + b
                    out[c, row : row + 1] += part[source : source + 1]
        for c in range(3):
            for a in range(4):
                source = 8 * a + level
                below = yb[c, source : source + 1]
                above = ya[c, source : source + 1]
                if side:
                    below = pltpu.roll(below, 121, 1)
                else:
                    above = pltpu.roll(above, 7, 1)
                out[c, 4 * a : 4 * a + 1] += jnp.where(lane == 0, below, 0.0)
                out[c, 4 * a + 3 : 4 * a + 4] += jnp.where(lane == 7, above, 0.0)


def end_kernel(adv_in, helm_in, xb, xa, yb, ya, zb, za, adv, helm, work, sems):
    loads, stores = [], []
    for c in range(3):
        for part, (source, target) in enumerate(((adv_in, adv), (helm_in, helm))):
            n = 2 * c + part
            loads.append(pltpu.make_async_copy(source.at[c], work.at[n], sems.at[n]))
            stores.append(pltpu.make_async_copy(work.at[n], target.at[c], sems.at[6 + n]))
            loads[n].start()
    lane = lane_iota((32, 128))
    level = lax.broadcasted_iota(jnp.int32, (16, 8, 512), 1)
    turned = [[got[...], pltpu.roll(got[...].reshape(-1, 128), 64, 1).reshape(got.shape)] for got in (xb, xa, yb, ya, zb, za)]
    for part in range(2):
        low_x, high_x = turned[0][part], turned[1][1 - part]
        wide = [spread(turned[2 + side][part].reshape(96, 128), pick_table(side)) for side in range(2)]
        ends = [spread(turned[4 + side][part].reshape(48, 128), pick_table(2 + side)) for side in range(2)]
        for c in range(3):
            n = 2 * c + part
            loads[n].wait()
            rows = slice(16 * c, 16 * c + 16)
            total = work[n].reshape(16, 8, 512)
            total = total + jnp.where(level == 0, ends[0][rows][:, None, :], 0.0)
            total = total + jnp.where(level == 7, ends[1][rows][:, None, :], 0.0)
            work[n] = total.reshape(128, 512)
            work[n, 0:32, 0:128] += jnp.where(lane < 64, low_x[c], 0.0)
            work[n, 96:128, 384:512] += jnp.where(lane >= 64, high_x[c], 0.0)
            for side, start in ((0, 0), (1, 24)):
                for a in range(4):
                    row = 32 * a + start
                    source = 32 * c + 8 * a
                    work[n, row : row + 8] += wide[side][source : source + 8]
            stores[n].start()
    for store in stores:
        store.wait()


def pack_kernel(coords, idents, counts, out):
    for source in range(32):
        for d in range(3):
            out[source, 4 * d : 4 * d + 4, 0] = coords[source, d]
    slot = lane_iota((32, 4))
    tags = jnp.where(slot < counts[...], idents[...], -1).astype(f32)
    out[:, 12, 0, 0:4] = tags


def table_kernel(vel, table):
    lane = lane_iota((128, 128))
    for c in range(3):
        for tile in range(4):
            x = vel[c, :, 128 * tile : 128 * tile + 128]
            high = x.astype(bf16).astype(f32)
            low = x - high
            for part in range(4):
                i, j_high = 2 * tile + part // 2, part % 2
                shift = -32 * part
                a = pltpu.roll(high, shift % 128, 1) if part else high
                b = pltpu.roll(low, (shift + 32) % 128, 1) if (shift + 32) % 128 else low
                d = pltpu.roll(high, (shift + 64) % 128, 1) if (shift + 64) % 128 else high
                row = (j_high * 3 + c) * 8 + i
                mixed = jnp.where(lane < 32, a, jnp.where(lane < 64, b, jnp.where(lane < 96, d, 0.0)))
                table[128 * row : 128 * row + 128] = mixed


def fibre_kernel(got_in, table, basis, got, out, live, tags, sem):
    load = pltpu.make_async_copy(got_in.at[:, 12, 0], tags, sem)
    load.start()
    load.wait()

    def ids(block):
        return tags[block // 4, block % 4]

    for slot in range(128 + UNROLL):
        live[slot] = 0

    def gather(block, count):
        live[count] = block
        return count + jnp.where(ids(block) >= 0.0, 1, 0)

    count = lax.fori_loop(0, 128, gather, 0, unroll=8)
    live[count] = 0

    def weights(position):
        value = basis[7]
        for place in range(7):
            value = value * (position - basis[place])
        return value

    def one(block):
        source = block // 4
        slot = block % 4
        elem = jnp.maximum(ids(block), 0.0).astype(jnp.int32)
        nodes = table[pl.ds(elem, 48, stride=128), :].astype(bf16)
        basis_x, basis_y, basis_z = (
            weights(jnp.broadcast_to(got[source, 4 * d + slot], (8, 128))) for d in range(3)
        )
        high = basis_z.astype(bf16).astype(f32)
        low = basis_z - high
        zero = jnp.zeros((8, 128), f32)
        columns = []
        for j in range(4):
            pieces = [zero] * 16
            pieces[j] = high
            pieces[4 + j] = high
            pieces[8 + j] = low
            columns.append(jnp.concatenate(pieces, 0).astype(bf16))
        sections = [mm(nodes, column) for column in columns]
        for c in range(3):
            total = jnp.zeros((8, 128), f32)
            for j in range(8):
                row = (j // 4 * 3 + c) * 8
                total = total + sections[j % 4][row : row + 8] * basis_y[j : j + 1]
            out[source, 4 * c + slot] = jnp.sum(total * basis_x, axis=0, keepdims=True)

    def group(step, carry):
        for u in range(UNROLL):
            one(live[step * UNROLL + u])
        return carry

    lax.fori_loop(0, (count + UNROLL - 1) // UNROLL, group, 0)


vmem = pl.BlockSpec(memory_space=pltpu.VMEM)
hbm = pl.BlockSpec(memory_space=pltpu.HBM)
anywhere = pl.BlockSpec(memory_space=pl.ANY)


def call(kernel, outs, args, specs=None, scratch=(), out_specs=None):
    out_specs = out_specs or [vmem] * len(outs)
    args = [
        pltpu.with_memory_space_constraint(arg, pltpu.HBM) if spec is hbm else arg
        for arg, spec in zip(args, specs or [vmem] * len(args))
    ]
    shapes = [
        pltpu.HBM(shape, f32) if spec is hbm else jax.ShapeDtypeStruct(shape, f32)
        for shape, spec in zip(outs, out_specs)
    ]
    return pl.pallas_call(
        kernel,
        out_shape=shapes,
        in_specs=specs or [vmem] * len(args),
        out_specs=out_specs,
        scratch_shapes=list(scratch),
        compiler_params=pltpu.CompilerParams(vmem_limit_bytes=VMEM_LIMIT),
        name=kernel.__name__,
    )(*args)


def swap(axis, left, right):
    size = lax.axis_size(axis)
    odd = lax.axis_index(axis) % 2 == 1
    even_pairs = [(i, i ^ 1) for i in range(size)]
    odd_pairs = [(i, ((i + 1) ^ 1) - 1) for i in range(1, size - 1)]
    first = lax.ppermute(jnp.where(odd, left, right), axis, even_pairs)
    second = lax.ppermute(jnp.where(odd, right, left), axis, odd_pairs)
    return jnp.where(odd, first, second), jnp.where(odd, second, first)


def body(velocity, viscosity, fibre_coords, fibre_elem, block_count, fibre_velocity):
    vel = velocity.reshape(3, 128, 512)
    visc = viscosity.reshape(128, 512)
    coords = fibre_coords.reshape(32, 4, 3, 128).transpose(0, 2, 1, 3)
    idents = fibre_elem.reshape(32, 4)
    counts = block_count.reshape(32, 1)
    own_velocity = fibre_velocity.reshape(32, 4, 3, 128).transpose(0, 2, 1, 3)
    live = lax.broadcasted_iota(jnp.int32, (32, 4), 1) < counts
    (packed,) = call(pack_kernel, [(32, 13, 1, 128)], (coords, idents, counts))
    got = lax.all_to_all(packed, "gz", split_axis=0, concat_axis=0, tiled=True)

    dx, dyz, mass = operator_tables()
    field = (3, 128, 512)
    y_face, z_face = (3, 32, 128), (3, 16, 128)
    adv, helm, xl, xr, yl, yr, zl, zr = call(
        fluid_kernel, [field, field] + [y_face] * 4 + [z_face] * 2, (vel, visc, dx, dyz, mass),
        specs=[hbm] * 5,
        out_specs=[hbm] * 2 + [vmem] * 6,
        scratch=[
            pltpu.VMEM((3, 384, 512), f32),
            pltpu.VMEM(field, f32),
            pltpu.VMEM(field, f32),
            pltpu.VMEM(field, f32),
            pltpu.VMEM((128, 512), f32),
            pltpu.VMEM(dx.shape, f32),
            pltpu.VMEM(dyz.shape, f32),
            pltpu.VMEM((1, 512), f32),
            pltpu.SemaphoreType.DMA((11,)),
        ],
    )
    (table,) = call(table_kernel, [(48 * 128, 128)], (vel,))
    xb, xa = swap("gx", xl, xr)
    yl, yr = call(y_face_kernel, [y_face] * 2, (xb, xa, yl, yr))
    yb, ya = swap("gy", yl, yr)
    got, yl = lax.optimization_barrier((got, yl))
    (values,) = call(
        fibre_kernel, [(32, 12, 1, 128)], (got, table, basis_table(), got),
        specs=[anywhere, vmem, vmem, vmem],
        scratch=[
            pltpu.SMEM((128 + 2 * UNROLL,), jnp.int32),
            pltpu.SMEM((32, 128), f32),
            pltpu.SemaphoreType.DMA,
        ],
    )
    values, yb, ya = lax.optimization_barrier((values, yb, ya))
    zl, zr = call(z_face_kernel, [z_face] * 2, (xb, xa, yb, ya, zl, zr))
    zb, za = swap("gz", zl, zr)
    adv, helm = call(
        end_kernel, [field, field], (adv, helm, xb, xa, yb, ya, zb, za),
        specs=[hbm] * 2 + [vmem] * 6, out_specs=[hbm] * 2,
        scratch=[
            pltpu.VMEM((6, 128, 512), f32),
            pltpu.SemaphoreType.DMA((12,)),
        ],
    )
    sampled = lax.all_to_all(values, "gz", split_axis=0, concat_axis=0, tiled=True).reshape(32, 3, 4, 128)
    relative = sampled - own_velocity
    factor = jnp.sqrt(1.0 + jnp.sum(relative * relative, axis=1, keepdims=True))
    drag = jnp.where(live[:, None, :, None], drag_scale * factor * relative, 0.0)
    drag = drag.transpose(0, 2, 1, 3).reshape(fibre_coords.shape)
    return adv.reshape(velocity.shape), helm.reshape(velocity.shape), drag


def solution(mesh):
    in_specs = (
        P(None, "gx", "gy", "gz", None),
        P("gx", "gy", "gz", None),
        P("gx", "gy", "gz", None, None, None, None),
        P("gx", "gy", "gz", None, None),
        P("gx", "gy", "gz", None),
        P("gx", "gy", "gz", None, None, None, None),
    )
    out_specs = (
        P(None, "gx", "gy", "gz", None),
        P(None, "gx", "gy", "gz", None),
        P("gx", "gy", "gz", None, None, None, None),
    )
    return jax.shard_map(body, mesh=mesh, in_specs=in_specs, out_specs=out_specs, check_vma=False)
```

time: 152 us -> 87.1 us (0.57)
  the two profiles are of different devices: /device:TPU:6 before, /device:TPU:20 now
where the time goes in v1:
time: 87.1 us; the launch traced here: 86.3 us
  starting transfers between devices  41.6 us (48%)
  waiting for transfers between devices  17.5 us (20%)
  Pallas kernels  17.2 us (20%)
  local copies, waits for them, and re-layouts  6.46 us (7%)
  other arithmetic  2.63 us (3%)
  between operations  0.9 us (1%)
    pallas_call x7, Pallas kernels, call(): pl.pallas_call(kernel, out_shape=shapes, in_specs=specs or [vmem] * len(a...  17.2 us
    all_to_all x1, starting transfers between devices, body(): got = lax.all_to_all(packed, 'gz', split_axis=0, concat_axis=0, tiled=True)  15.5 us
    all_to_all x1, starting transfers between devices, body(): lax.all_to_all(values, 'gz', split_axis=0, concat_axis=0, tiled=True)  13.1 us
    all_to_all x1, waiting for transfers between devices, body(): lax.all_to_all(values, 'gz', split_axis=0, concat_axis=0, tiled=True)  11.5 us
    ppermute x3, starting transfers between devices, swap(): first = lax.ppermute(jnp.where(odd, left, right), axis, even_pairs)  8.48 us
    ppermute x3, waiting for transfers between devices, swap(): second = lax.ppermute(jnp.where(odd, right, left), axis, odd_pairs)  5.01 us
    unnamed x18, local copies, waits for them, and re-layouts  4.96 us
    ppermute x3, starting transfers between devices, swap(): second = lax.ppermute(jnp.where(odd, right, left), axis, odd_pairs)  4.5 us
  transfers between devices with their start and end apart: 8, of which 4 were waited for; matrix products, arithmetic and copies ran while one was open for 1% of the time, Pallas kernels for 14%

profile of v1, /device:TPU:20, one launch (start us, length us, event | category | flops | bytes accessed | tf_op | source)
XLA Modules:
  0.0 86.3 jit_solution(17259058347846984011)
XLA Ops:
  0.6 0.8 copy.13.idents
  1.4 0.7 copy.14.counts
  2.1 0.0 copy-start.2
  2.1 0.9 %copy-done.2 = f32[1,1,1,32,4,3,128]{6,4,5,3,2,1,0:T(4,128)S(1)} copy-done((f32[1,1,1,32,4,3,128]{6,4,5,3,2,1,0:T(4,128)S(1)}, f32[1,1,1,32,4,3,128]{6,4,5,3,2,1,0:T(4,128)}, u32[]{:S(2)}) %copy-start.2) | copy-done | bytes 196632
  3.1 0.8 pack_kernel.1
  3.9 15.5 %all-to-all-start = ((f32[32,13,1,128]{3,2,1,0:T(1,128)}), f32[32,13,1,128]{3,2,1,0:T(1,128)S(1)}, u32[]{:S(2)}, u32[]{:S(2)}) async-start(f32[32,13,1,128]{3,2,1,0:T(1,128)} %pack_kernel.1), calls=%async_computation | async-start | bytes 425984 | tf_op jit(solution)/shard_map/all_to_all | solution.py:421
  19.4 7.2 %fluid_kernel.1 = (f32[3,128,512]{2,1,0:T(8,128)}, f32[3,128,512]{2,1,0:T(8,128)}, f32[3,32,128]{2,1,0:T(8,128)S(1)}, f32[3,32,128]{2,1,0:T(8,128)S(1)}, f32[3,3...) custom-call(f32[3,128,512]{2,1,0:T(8,128)} %bitcast.23, ...), custom_call_target="tpu_custom_call" | custom-call | tf_op jit(solution)/shard_map/fluid_kernel/pallas_call | solution.py:391
  26.6 0.0 copy-start.4
  26.6 0.0 copy-start.6
  26.7 3.1 %collective-permute-start = (f32[3,32,128]{2,1,0:T(8,128)S(1)}, f32[3,32,128]{2,1,0:T(8,128)S(1)}, u32[]{:S(2)}, u32[]{:S(2)}) collective-permute-start(f32[3,32,128]{2,1,0:T(8,128)S(1)} %get-tuple-element.46), channel_id=1, source_target_pairs={{0,128},{128,0},{256,384},{384,256},{1,129},{129,1},{257,385},{385... | collective-permute-start | bytes 147464 | tf_op jit(solution)/shard_map/ppermute | solution.py:407
  29.8 1.9 %collective-permute-start.1 = (f32[3,32,128]{2,1,0:T(8,128)S(1)}, f32[3,32,128]{2,1,0:T(8,128)S(1)}, u32[]{:S(2)}, u32[]{:S(2)}) collective-permute-start(f32[3,32,128]{2,1,0:T(8,128)S(1)} %get-tuple-element.45), channel_id=1, source_target_pairs={{128,256},{256,128},{129,257},{257,129},{130,258},{258,130},{131,2... | collective-permute-start | bytes 147464 | tf_op jit(solution)/shard_map/ppermute | solution.py:408
  31.7 0.9 %collective-permute-done = f32[3,32,128]{2,1,0:T(8,128)S(1)} collective-permute-done((f32[3,32,128]{2,1,0:T(8,128)S(1)}, f32[3,32,128]{2,1,0:T(8,128)S(1)}, u32[]{:S(2)}, u32[]{:S(2)}) %collective-permute-start) | collective-permute-done | bytes 49184 | tf_op jit(solution)/shard_map/ppermute | solution.py:407
  32.6 0.0 copy-done.4
  32.6 0.0 copy-done.6
  32.6 3.1 %collective-permute-done.1 = f32[3,32,128]{2,1,0:T(8,128)S(1)} collective-permute-done((f32[3,32,128]{2,1,0:T(8,128)S(1)}, f32[3,32,128]{2,1,0:T(8,128)S(1)}, u32[]{:S(2)}, u32[]{:S(2)}) %collective-permute-start.1) | collective-permute-done | bytes 49184 | tf_op jit(solution)/shard_map/ppermute | solution.py:408
  35.8 0.1 y_face_kernel.1
  35.9 3.2 %collective-permute-start.2 = (f32[3,32,128]{2,1,0:T(8,128)S(1)}, f32[3,32,128]{2,1,0:T(8,128)S(1)}, u32[]{:S(2)}, u32[]{:S(2)}) collective-permute-start(f32[3,32,128]{2,1,0:T(8,128)S(1)} %get-tuple-element.42), channel_id=1, source_target_pairs={{0,32},{32,0},{64,96},{96,64},{1,33},{33,1},{65,97},{97,65},{2,34}... | collective-permute-start | bytes 147464 | tf_op jit(solution)/shard_map/ppermute | solution.py:407
  39.1 1.9 %collective-permute-start.3 = (f32[3,32,128]{2,1,0:T(8,128)S(1)}, f32[3,32,128]{2,1,0:T(8,128)S(1)}, u32[]{:S(2)}, u32[]{:S(2)}) collective-permute-start(f32[3,32,128]{2,1,0:T(8,128)S(1)} %get-tuple-element.41), channel_id=1, source_target_pairs={{32,64},{64,32},{33,65},{65,33},{34,66},{66,34},{35,67},{67,35},{3... | collective-permute-start | bytes 147464 | tf_op jit(solution)/shard_map/ppermute | solution.py:408
  41.0 0.0 copy-start
  41.0 1.1 %copy-done = f32[3,4,4,8,512]{4,3,2,1,0:T(8,128)S(1)} copy-done((f32[3,4,4,8,512]{4,3,2,1,0:T(8,128)S(1)}, f32[3,4,4,8,512]{4,3,2,1,0:T(8,128)}, u32[]{:S(2)}) %copy-start) | copy-done | bytes 786456
  42.1 1.0 %table_kernel.1.table = f32[6144,128]{1,0:T(8,128)S(1)} custom-call(f32[3,128,512]{2,1,0:T(8,128)S(1)} %bitcast.24), custom_call_target="tpu_custom_call" | custom-call | tf_op jit(solution)/shard_map/table_kernel/pallas_call | solution.py:391
  43.1 0.0 collective-permute-done.2
  43.2 1.9 %collective-permute-done.3 = f32[3,32,128]{2,1,0:T(8,128)S(1)} collective-permute-done((f32[3,32,128]{2,1,0:T(8,128)S(1)}, f32[3,32,128]{2,1,0:T(8,128)S(1)}, u32[]{:S(2)}, u32[]{:S(2)}) %collective-permute-start.3) | collective-permute-done | bytes 49184 | tf_op jit(solution)/shard_map/ppermute | solution.py:408
  45.1 0.0 all-to-all-done.got_in.got
  45.1 0.0 copy-start.3
  45.1 0.7 copy-done.3
  45.8 4.6 %fibre_kernel.1 = f32[32,12,1,128]{3,2,1,0:T(1,128)S(1)} custom-call(f32[32,13,1,128]{3,2,1,0:T(1,128)S(1)} %all-to-all-done.got_in.got, f32[6144,128]{1,0:T(8,128)S(1)} %table_kernel.1.table, f32[8,8,128]{2,1,0:T(8,128)S(1)} %copy-done.3, f32[32,13,1,128]{3,2,1,0:T(1,128)S(1)} %all-to-all-done.got_in.got), custom_call_target="tpu_custom_call" | custom-call | tf_op jit(solution)/shard_map/fibre_kernel/pallas_call | solution.py:391
  50.4 0.0 copy-start.1
  50.4 0.7 copy-done.1
  51.1 0.0 copy-start.8
  51.1 13.1 %all-to-all-start.1 = ((f32[32,12,1,128]{3,2,1,0:T(1,128)}), f32[32,12,1,128]{3,2,1,0:T(1,128)S(1)}, u32[]{:S(2)}, u32[]{:S(2)}) async-start(f32[32,12,1,128]{3,2,1,0:T(1,128)} %copy-done.1), calls=%async_computation.1 | async-start | bytes 393216 | tf_op jit(solution)/shard_map/all_to_all | solution.py:467
  64.3 0.0 copy-start.5
  64.3 0.7 copy-done.5
  65.0 0.0 copy-start.7
  65.0 0.7 copy-done.7
  65.7 0.2 z_face_kernel.1
  66.0 2.2 %collective-permute-start.4 = (f32[3,16,128]{2,1,0:T(8,128)S(1)}, f32[3,16,128]{2,1,0:T(8,128)S(1)}, u32[]{:S(2)}, u32[]{:S(2)}) collective-permute-start(f32[3,16,128]{2,1,0:T(8,128)S(1)} %get-tuple-element.50), channel_id=1, source_target_pairs={{0,1},{1,0},{2,3},{3,2},{4,5},{5,4},{6,7},{7,6},{8,9},{9,8},{10,11... | collective-permute-start | bytes 73736 | tf_op jit(solution)/shard_map/ppermute | solution.py:407
  68.2 0.7 collective-permute-start.5
  68.9 0.7 iota_compare_fusion
  69.6 0.0 collective-permute-done.4
  69.6 0.0 collective-permute-done.5
  69.6 3.3 %end_kernel.1 = (f32[3,128,512]{2,1,0:T(8,128)}, f32[3,128,512]{2,1,0:T(8,128)}) custom-call(f32[3,128,512]{2,1,0:T(8,128)} %get-tuple-element.21.adv_in, f32[3,128,512]{2,1,0:T(8,128)} %get-tuple-element.22.helm_in, f32[3,32,128]{2,1,0:T(8,128)S(1)} %get-tuple-element.44.xb, f32[3,32,128]{2,1,0:T(8,128)S(1)} %get-tuple-element.43.xa, ...), custom_call_target="tpu_custom_call" | custom-call | tf_op jit(solution)/shard_map/end_kernel/pallas_call | solution.py:391
  72.9 11.5 %all-to-all-done.1 = f32[32,12,1,128]{3,2,1,0:T(1,128)S(1)} async-done(((f32[32,12,1,128]{3,2,1,0:T(1,128)}), f32[32,12,1,128]{3,2,1,0:T(1,128)S(1)}, u32[]{:S(2)}, u32[]{:S(2)}) %all-to-all-start.1) | async-done | bytes 196640 | tf_op jit(solution)/shard_map/all_to_all | solution.py:467
  84.4 1.0 %multiply_reduce_fusion = f32[32,4,128]{2,1,0:T(4,128)S(1)} fusion(f32[32,3,4,128]{3,2,1,0:T(4,128)S(1)} %bitcast.26, f32[1,1,1,32,4,3,128]{6,4,5,3,2,1,0:T(4,128)} %param.15), kind=kLoop, calls=%fused_computation.2 | loop fusion | flops 131072 | bytes 458752 | tf_op jit(solution)/shard_map/reduce_sum | solution.py:469
  85.5 0.0 copy-done.8
  85.5 0.8 select_bitcast_fusion
  (7 shorter events, 0.1 us)
Async XLA Ops:
  2.1 0.9 %copy-start.2 = (f32[1,1,1,32,4,3,128]{6,4,5,3,2,1,0:T(4,128)S(1)}, f32[1,1,1,32,4,3,128]{6,4,5,3,2,1,0:T(4,128)}, u32[]{:S(2)}) copy-start(f32[1,1,1,32,4,3,128]{6,4,5,3,2,1,0:T(4,128)} %param.12) | copy-start | bytes 589828
  3.9 41.2 %all-to-all-start = ((f32[32,13,1,128]{3,2,1,0:T(1,128)}), f32[32,13,1,128]{3,2,1,0:T(1,128)S(1)}, u32[]{:S(2)}, u32[]{:S(2)}) async-start(f32[32,13,1,128]{3,2,1,0:T(1,128)} %pack_kernel.1), calls=%async_computation | async-start | bytes 425984 | tf_op jit(solution)/shard_map/all_to_all | solution.py:421
  26.6 6.0 %copy-start.4 = (f32[3,16,128]{2,1,0:T(8,128)}, f32[3,16,128]{2,1,0:T(8,128)S(1)}, u32[]{:S(2)}) copy-start(f32[3,16,128]{2,1,0:T(8,128)S(1)} %get-tuple-element.32.zl_in) | copy-start | bytes 73732
  26.6 6.0 %copy-start.6 = (f32[3,16,128]{2,1,0:T(8,128)}, f32[3,16,128]{2,1,0:T(8,128)S(1)}, u32[]{:S(2)}) copy-start(f32[3,16,128]{2,1,0:T(8,128)S(1)} %get-tuple-element.33.zr_in) | copy-start | bytes 73732
  26.7 6.0 %collective-permute-start = (f32[3,32,128]{2,1,0:T(8,128)S(1)}, f32[3,32,128]{2,1,0:T(8,128)S(1)}, u32[]{:S(2)}, u32[]{:S(2)}) collective-permute-start(f32[3,32,128]{2,1,0:T(8,128)S(1)} %get-tuple-element.46), channel_id=1, source_target_pairs={{0,128},{128,0},{256,384},{384,256},{1,129},{129,1},{257,385},{385... | collective-permute-start | bytes 147464 | tf_op jit(solution)/shard_map/ppermute | solution.py:407
  29.8 6.0 %collective-permute-start.1 = (f32[3,32,128]{2,1,0:T(8,128)S(1)}, f32[3,32,128]{2,1,0:T(8,128)S(1)}, u32[]{:S(2)}, u32[]{:S(2)}) collective-permute-start(f32[3,32,128]{2,1,0:T(8,128)S(1)} %get-tuple-element.45), channel_id=1, source_target_pairs={{128,256},{256,128},{129,257},{257,129},{130,258},{258,130},{131,2... | collective-permute-start | bytes 147464 | tf_op jit(solution)/shard_map/ppermute | solution.py:408
  35.9 7.3 %collective-permute-start.2 = (f32[3,32,128]{2,1,0:T(8,128)S(1)}, f32[3,32,128]{2,1,0:T(8,128)S(1)}, u32[]{:S(2)}, u32[]{:S(2)}) collective-permute-start(f32[3,32,128]{2,1,0:T(8,128)S(1)} %get-tuple-element.42), channel_id=1, source_target_pairs={{0,32},{32,0},{64,96},{96,64},{1,33},{33,1},{65,97},{97,65},{2,34}... | collective-permute-start | bytes 147464 | tf_op jit(solution)/shard_map/ppermute | solution.py:407
  39.1 6.0 %collective-permute-start.3 = (f32[3,32,128]{2,1,0:T(8,128)S(1)}, f32[3,32,128]{2,1,0:T(8,128)S(1)}, u32[]{:S(2)}, u32[]{:S(2)}) collective-permute-start(f32[3,32,128]{2,1,0:T(8,128)S(1)} %get-tuple-element.41), channel_id=1, source_target_pairs={{32,64},{64,32},{33,65},{65,33},{34,66},{66,34},{35,67},{67,35},{3... | collective-permute-start | bytes 147464 | tf_op jit(solution)/shard_map/ppermute | solution.py:408
  41.0 1.1 %copy-start = (f32[3,4,4,8,512]{4,3,2,1,0:T(8,128)S(1)}, f32[3,4,4,8,512]{4,3,2,1,0:T(8,128)}, u32[]{:S(2)}) copy-start(f32[3,4,4,8,512]{4,3,2,1,0:T(8,128)} %param.10) | copy-start | bytes 2359300
  45.1 0.8 copy-start.3
  50.4 0.7 copy-start.1
  51.1 34.4 %copy-start.8 = (f32[1,1,1,32,4,3,128]{6,4,5,3,2,1,0:T(4,128)S(1)}, f32[1,1,1,32,4,3,128]{6,4,5,3,2,1,0:T(4,128)}, u32[]{:S(2)}) copy-start(f32[1,1,1,32,4,3,128]{6,4,5,3,2,1,0:T(4,128)} %param.15) | copy-start | bytes 589828
  51.1 33.3 %all-to-all-start.1 = ((f32[32,12,1,128]{3,2,1,0:T(1,128)}), f32[32,12,1,128]{3,2,1,0:T(1,128)S(1)}, u32[]{:S(2)}, u32[]{:S(2)}) async-start(f32[32,12,1,128]{3,2,1,0:T(1,128)} %copy-done.1), calls=%async_computation.1 | async-start | bytes 393216 | tf_op jit(solution)/shard_map/all_to_all | solution.py:467
  64.3 0.7 copy-start.5
  65.0 0.7 copy-start.7
  66.0 3.6 %collective-permute-start.4 = (f32[3,16,128]{2,1,0:T(8,128)S(1)}, f32[3,16,128]{2,1,0:T(8,128)S(1)}, u32[]{:S(2)}, u32[]{:S(2)}) collective-permute-start(f32[3,16,128]{2,1,0:T(8,128)S(1)} %get-tuple-element.50), channel_id=1, source_target_pairs={{0,1},{1,0},{2,3},{3,2},{4,5},{5,4},{6,7},{7,6},{8,9},{9,8},{10,11... | collective-permute-start | bytes 73736 | tf_op jit(solution)/shard_map/ppermute | solution.py:407
  68.2 1.4 %collective-permute-start.5 = (f32[3,16,128]{2,1,0:T(8,128)S(1)}, f32[3,16,128]{2,1,0:T(8,128)S(1)}, u32[]{:S(2)}, u32[]{:S(2)}) collective-permute-start(f32[3,16,128]{2,1,0:T(8,128)S(1)} %get-tuple-element.49), channel_id=1, source_target_pairs={{1,2},{2,1},{3,4},{4,3},{5,6},{6,5},{7,8},{8,7},{9,10},{10,9},{11,... | collective-permute-start | bytes 73736 | tf_op jit(solution)/shard_map/ppermute | solution.py:408

commit v2 on v1

--- a/solution.py
+++ b/solution.py
@@ -89,16 +89,22 @@
     return jnp.where(hit, 1.0, 0.0).astype(bf16)
 
 
-def basis_table():
-    table = np.zeros((8, 8, 128))
-    for node in range(8):
-        others = [other for other in range(8) if other != node]
+def basis_rows():
+    node = lax.broadcasted_iota(jnp.int32, (8, 128), 0)
+    rows = []
+    for place in range(7):
+        value = jnp.full((8, 128), gll_points[place + 1], f32)
+        for row in range(place + 1, 8):
+            value = jnp.where(node == row, gll_points[place], value)
+        rows.append(value)
+    scales = jnp.ones((8, 128), f32)
+    for row in range(8):
         scale = 1.0
-        for place, other in enumerate(others):
-            table[place, node] = gll_points[other]
-            scale = scale / (gll_points[node] - gll_points[other])
-        table[7, node] = scale
-    return table.astype(np.float32)
+        for other in range(8):
+            if other != row:
+                scale = scale / (gll_points[row] - gll_points[other])
+        scales = jnp.where(node == row, scale, scales)
+    return rows, scales
 
 
 def split(x):
@@ -132,12 +138,13 @@
     return lax.broadcasted_iota(jnp.int32, shape, len(shape) - 1)
 
 
-def fluid_kernel(vel_in, visc_in, dx_in, dyz_in, mass_in, adv_out, helm_out, xl, xr, yl, yr, zl, zr, flux, adv, helm, vel, visc, dx_ref, dyz_ref, mass_ref, sems):
+def fluid_kernel(odds, vel_in, visc_in, dx_in, dyz_in, mass_in, adv_out, helm_out, x_work, y_out, z_out, table, flux, y_work, z_work, adv, helm, vel, visc, dx_ref, dyz_ref, mass_ref, sems):
     pairs = ((vel_in, vel), (dx_in, dx_ref), (dyz_in, dyz_ref), (visc_in, visc), (mass_in, mass_ref))
     loads = [pltpu.make_async_copy(a, b, sems.at[n]) for n, (a, b) in enumerate(pairs)]
     for load in loads:
         load.start()
     loads[0].wait()
+    fill_table(vel, table, (0, 1))
     loads[1].wait()
     v = vel[...].reshape(384, 512)
     dx = split(dx_ref[...])
@@ -172,21 +179,29 @@
             stores.append(pltpu.make_async_copy(field.at[c], out.at[c], sems.at[5 + len(stores)]))
             stores[-1].start()
     lane = lane_iota((32, 128))
+    odd = odds[0]
     for c in range(3):
-        xl[c] = jnp.where(lane < 64, adv[c, 0:32, 0:128], pltpu.roll(helm[c, 0:32, 0:128], 64, 1))
-        xr[c] = jnp.where(lane < 64, pltpu.roll(adv[c, 96:128, 384:512], 64, 1), helm[c, 96:128, 384:512])
-    for out, start, side in ((yl, 0, 0), (yr, 24, 1)):
+        left = jnp.where(lane < 64, adv[c, 0:32, 0:128], pltpu.roll(helm[c, 0:32, 0:128], 64, 1))
+        right = jnp.where(lane < 64, pltpu.roll(adv[c, 96:128, 384:512], 64, 1), helm[c, 96:128, 384:512])
+        x_work[1 - odd, c] = left
+        x_work[odd, c] = right
+    for out, start, side in ((y_work.at[0], 0, 0), (y_work.at[1], 24, 1)):
         faces = []
         for field in (adv, helm):
             rows = field[...].reshape(12, 32, 512)[:, start : start + 8].reshape(96, 512)
             faces.append(pick(rows, pick_table(side)))
         out[...] = (faces[0] + pltpu.roll(faces[1], 64, 1)).reshape(3, 32, 128)
-    for out, start, side in ((zl, 0, 2), (zr, 7, 3)):
+    for out, start, side in ((z_work.at[0], 0, 2), (z_work.at[1], 7, 3)):
         faces = []
         for field in (adv, helm):
             rows = field[...].reshape(48, 8, 512)[:, start]
             faces.append(pick(rows, pick_table(side)))
         out[...] = (faces[0] + pltpu.roll(faces[1], 64, 1)).reshape(3, 16, 128)
+    stores.append(pltpu.make_async_copy(y_work, y_out, sems.at[12]))
+    stores[-1].start()
+    stores.append(pltpu.make_async_copy(z_work, z_out, sems.at[13]))
+    stores[-1].start()
+    fill_table(vel, table, (2, 3))
     for store in stores:
         store.wait()
 
@@ -217,90 +232,161 @@
         field[c, :, lanes] = z.reshape(128, 128)
 
 
-def y_face_kernel(xb, xa, yl_in, yr_in, yl, yr):
+def both_sides(odd, first, second):
+    flag = jnp.full((8, 128), odd, jnp.int32) == 1
+
+    def below(c, rows):
+        flags = flag[: rows.stop - rows.start]
+        return jnp.where(flags, first[c, rows], second[c, rows])
+
+    def above(c, rows):
+        flags = flag[: rows.stop - rows.start]
+        return jnp.where(flags, second[c, rows], first[c, rows])
+
+    return below, above
+
+
+def y_face_kernel(odds, x1_in, x2_in, y_in, z_in, y1, y2, x1, x2, z, y_raw, sems):
+    pairs = ((x1_in, x1), (x2_in, x2), (y_in, y_raw), (z_in, z))
+    loads = [pltpu.make_async_copy(a, b, sems.at[n]) for n, (a, b) in enumerate(pairs)]
+    for load in loads:
+        load.start()
+    for load in loads:
+        load.wait()
     lane = lane_iota((8, 128)) % 64
+    xb, xa = both_sides(odds[0], x1, x2)
+    odd = jnp.full((8, 128), odds[1], jnp.int32) == 1
+    head, tail = slice(0, 8), slice(24, 32)
     for c in range(3):
-        yl[c, 0:8] = yl_in[c, 0:8] + jnp.where(lane < 8, xb[c, 0:8], 0.0)
-        yr[c, 0:8] = yr_in[c, 0:8] + jnp.where(lane < 8, pltpu.roll(xb[c, 24:32], 72, 1), 0.0)
-        yl[c, 8:24] = yl_in[c, 8:24]
-        yr[c, 8:24] = yr_in[c, 8:24]
-        yl[c, 24:32] = yl_in[c, 24:32] + jnp.where(lane >= 56, pltpu.roll(xa[c, 0:8], 56, 1), 0.0)
-        yr[c, 24:32] = yr_in[c, 24:32] + jnp.where(lane >= 56, xa[c, 24:32], 0.0)
-
-
-def z_face_kernel(xb, xa, yb, ya, zl_in, zr_in, zl, zr):
-    zl[...] = zl_in[...]
-    zr[...] = zr_in[...]
+        extra = {
+            (0, 0): jnp.where(lane < 8, xb(c, head), 0.0),
+            (1, 0): jnp.where(lane < 8, pltpu.roll(xb(c, tail), 72, 1), 0.0),
+            (0, 3): jnp.where(lane >= 56, pltpu.roll(xa(c, head), 56, 1), 0.0),
+            (1, 3): jnp.where(lane >= 56, xa(c, tail), 0.0),
+        }
+        for a in range(4):
+            rows = slice(8 * a, 8 * a + 8)
+            left, right = y_raw[0, c, rows], y_raw[1, c, rows]
+            if a in (0, 3):
+                left = left + extra[0, a]
+                right = right + extra[1, a]
+            y1[c, rows] = jnp.where(odd, left, right)
+            y2[c, rows] = jnp.where(odd, right, left)
+
+
+def z_face_kernel(odds, x1, x2, y1, y2, z_raw, out1, out2, z):
+    z[...] = z_raw[...]
     lane = lane_iota((1, 128)) % 8
-    for out, level, side in ((zl, 0, 0), (zr, 7, 1)):
+    x_odd = jnp.full((96, 128), odds[0], jnp.int32) == 1
+    x_first, x_second = x1[...].reshape(96, 128), x2[...].reshape(96, 128)
+    xb, xa = jnp.where(x_odd, x_first, x_second), jnp.where(x_odd, x_second, x_first)
+    yb, ya = both_sides(odds[1], y1, y2)
+    for level, side in ((0, 0), (7, 1)):
         for got, place in ((xb, 0), (xa, 1)):
-            part = pick(got[...].reshape(96, 128), edge_table(side, place))
+            part = pick(got, edge_table(side, place))
             for c in range(3):
                 for b in range(4):
                     source = 32 * c + 8 * b + level
                     row = 12 * place + b
-                    out[c, row : row + 1] += part[source : source + 1]
+                    z[side, c, row : row + 1] += part[source : source + 1]
         for c in range(3):
             for a in range(4):
-                source = 8 * a + level
-                below = yb[c, source : source + 1]
-                above = ya[c, source : source + 1]
+                row = slice(8 * a + level, 8 * a + level + 1)
+                below, above = yb(c, row), ya(c, row)
                 if side:
                     below = pltpu.roll(below, 121, 1)
                 else:
                     above = pltpu.roll(above, 7, 1)
-                out[c, 4 * a : 4 * a + 1] += jnp.where(lane == 0, below, 0.0)
-                out[c, 4 * a + 3 : 4 * a + 4] += jnp.where(lane == 7, above, 0.0)
-
-
-def end_kernel(adv_in, helm_in, xb, xa, yb, ya, zb, za, adv, helm, work, sems):
-    loads, stores = [], []
+                z[side, c, 4 * a : 4 * a + 1] += jnp.where(lane == 0, below, 0.0)
+                z[side, c, 4 * a + 3 : 4 * a + 4] += jnp.where(lane == 7, above, 0.0)
+    odd = jnp.full((3, 16, 128), odds[2], jnp.int32) == 1
+    out1[...] = jnp.where(odd, z[0], z[1])
+    out2[...] = jnp.where(odd, z[1], z[0])
+
+
+def sides(odd, first, second):
+    rows = first.shape[0] * first.shape[1]
+    flag = jnp.full((rows, 128), odd, jnp.int32) == 1
+    one, two = first[...].reshape(rows, 128), second[...].reshape(rows, 128)
+    below, above = jnp.where(flag, one, two), jnp.where(flag, two, one)
+    return [[got, pltpu.roll(got, 64, 1)] for got in (below, above)]
+
+
+def side_kernel(odds, adv_in, helm_in, x1, x2, y1, y2, work, sems):
+    loads = []
     for c in range(3):
-        for part, (source, target) in enumerate(((adv_in, adv), (helm_in, helm))):
-            n = 2 * c + part
+        for part, source in enumerate((adv_in, helm_in)):
+            n = 3 * part + c
             loads.append(pltpu.make_async_copy(source.at[c], work.at[n], sems.at[n]))
-            stores.append(pltpu.make_async_copy(work.at[n], target.at[c], sems.at[6 + n]))
-            loads[n].start()
+            loads[-1].start()
     lane = lane_iota((32, 128))
+    x_sides = sides(odds[0], x1, x2)
+    y_sides = sides(odds[1], y1, y2)
+    wide = [[spread(y_sides[side][part], pick_table(side)) for side in range(2)] for part in range(2)]
+    for load in loads:
+        load.wait()
+    for part in range(2):
+        for c in range(3):
+            n = 3 * part + c
+            faces = slice(32 * c, 32 * c + 32)
+            work[n, 0:32, 0:128] += jnp.where(lane < 64, x_sides[0][part][faces], 0.0)
+            work[n, 96:128, 384:512] += jnp.where(lane >= 64, x_sides[1][1 - part][faces], 0.0)
+            for side, start in ((0, 0), (1, 24)):
+                for a in range(4):
+                    row = 32 * a + start
+                    source = 32 * c + 8 * a
+                    work[n, row : row + 8] += wide[part][side][source : source + 8]
+
+
+def end_kernel(odds, work, z1, z2, adv, helm, done, sems):
     level = lax.broadcasted_iota(jnp.int32, (16, 8, 512), 1)
-    turned = [[got[...], pltpu.roll(got[...].reshape(-1, 128), 64, 1).reshape(got.shape)] for got in (xb, xa, yb, ya, zb, za)]
-    for part in range(2):
-        low_x, high_x = turned[0][part], turned[1][1 - part]
-        wide = [spread(turned[2 + side][part].reshape(96, 128), pick_table(side)) for side in range(2)]
-        ends = [spread(turned[4 + side][part].reshape(48, 128), pick_table(2 + side)) for side in range(2)]
+    z_sides = sides(odds[2], z1, z2)
+    stores = []
+    for part, target in enumerate((adv, helm)):
+        ends = [spread(z_sides[side][part], pick_table(2 + side)) for side in range(2)]
         for c in range(3):
-            n = 2 * c + part
-            loads[n].wait()
+            n = 3 * part + c
             rows = slice(16 * c, 16 * c + 16)
             total = work[n].reshape(16, 8, 512)
             total = total + jnp.where(level == 0, ends[0][rows][:, None, :], 0.0)
             total = total + jnp.where(level == 7, ends[1][rows][:, None, :], 0.0)
-            work[n] = total.reshape(128, 512)
-            work[n, 0:32, 0:128] += jnp.where(lane < 64, low_x[c], 0.0)
-            work[n, 96:128, 384:512] += jnp.where(lane >= 64, high_x[c], 0.0)
-            for side, start in ((0, 0), (1, 24)):
-                for a in range(4):
-                    row = 32 * a + start
-                    source = 32 * c + 8 * a
-                    work[n, row : row + 8] += wide[side][source : source + 8]
-            stores[n].start()
+            done[n] = total.reshape(128, 512)
+            stores.append(pltpu.make_async_copy(done.at[n], target.at[c], sems.at[n]))
+            stores[-1].start()
     for store in stores:
         store.wait()
 
 
-def pack_kernel(coords, idents, counts, out):
+def drag_kernel(counts, sampled, own, out):
+    slot = lax.broadcasted_iota(jnp.int32, (4, 128), 0)
+    for source in range(32):
+        relative = [sampled[source, 4 * d : 4 * d + 4, 0] - own[source, d] for d in range(3)]
+        square = relative[0] * relative[0] + relative[1] * relative[1] + relative[2] * relative[2]
+        factor = jnp.where(slot < counts[source], drag_scale * jnp.sqrt(1.0 + square), 0.0)
+        for d in range(3):
+            out[source, d] = jnp.where(slot < counts[source], factor * relative[d], 0.0)
+
+
+def pack_kernel(coords_in, idents_in, counts_in, out, coords, idents, counts, sems):
+    pairs = ((coords_in, coords), (idents_in, idents), (counts_in, counts))
+    loads = [pltpu.make_async_copy(a, b, sems.at[n]) for n, (a, b) in enumerate(pairs)]
+    for load in loads:
+        load.start()
+    for load in loads:
+        load.wait()
+    slot = lax.broadcasted_iota(jnp.int32, (4, 32), 0)
+    tags = jnp.where(slot < counts[...], idents[...], -1).astype(f32)
+    tags = jnp.concatenate([tags[q : q + 1] for q in range(4)], axis=1)
     for source in range(32):
         for d in range(3):
             out[source, 4 * d : 4 * d + 4, 0] = coords[source, d]
-    slot = lane_iota((32, 4))
-    tags = jnp.where(slot < counts[...], idents[...], -1).astype(f32)
-    out[:, 12, 0, 0:4] = tags
-
-
-def table_kernel(vel, table):
+        out[source, 12] = tags
+
+
+def fill_table(vel, table, tiles):
     lane = lane_iota((128, 128))
     for c in range(3):
-        for tile in range(4):
+        for tile in tiles:
             x = vel[c, :, 128 * tile : 128 * tile + 128]
             high = x.astype(bf16).astype(f32)
             low = x - high
@@ -315,13 +401,16 @@
                 table[128 * row : 128 * row + 128] = mixed
 
 
-def fibre_kernel(got_in, table, basis, got, out, live, tags, sem):
-    load = pltpu.make_async_copy(got_in.at[:, 12, 0], tags, sem)
-    load.start()
-    load.wait()
+def fibre_kernel(place, got_in, table, out_hbm, got, out, live, tags, sems):
+    load_tags = pltpu.make_async_copy(got_in.at[:, 12, 0], tags, sems.at[0])
+    load_tags.start()
+    load_got = pltpu.make_async_copy(got_in, got, sems.at[1])
+    load_got.start()
+    load_tags.wait()
+    me = place[0]
 
     def ids(block):
-        return tags[block // 4, block % 4]
+        return tags[block // 4, block % 4 * 32 + me]
 
     for slot in range(128 + UNROLL):
         live[slot] = 0
@@ -332,11 +421,13 @@
 
     count = lax.fori_loop(0, 128, gather, 0, unroll=8)
     live[count] = 0
+    load_got.wait()
+    rows, scales = basis_rows()
 
     def weights(position):
-        value = basis[7]
-        for place in range(7):
-            value = value * (position - basis[place])
+        value = scales
+        for row in rows:
+            value = value * (position - row)
         return value
 
     def one(block):
@@ -361,8 +452,8 @@
         for c in range(3):
             total = jnp.zeros((8, 128), f32)
             for j in range(8):
-                row = (j // 4 * 3 + c) * 8
-                total = total + sections[j % 4][row : row + 8] * basis_y[j : j + 1]
+                top = (j // 4 * 3 + c) * 8
+                total = total + sections[j % 4][top : top + 8] * basis_y[j : j + 1]
             out[source, 4 * c + slot] = jnp.sum(total * basis_x, axis=0, keepdims=True)
 
     def group(step, carry):
@@ -371,11 +462,14 @@
         return carry
 
     lax.fori_loop(0, (count + UNROLL - 1) // UNROLL, group, 0)
+    store = pltpu.make_async_copy(out, out_hbm, sems.at[2])
+    store.start()
+    store.wait()
 
 
 vmem = pl.BlockSpec(memory_space=pltpu.VMEM)
 hbm = pl.BlockSpec(memory_space=pltpu.HBM)
-anywhere = pl.BlockSpec(memory_space=pl.ANY)
+smem = pl.BlockSpec(memory_space=pltpu.SMEM)
 
 
 def call(kernel, outs, args, specs=None, scratch=(), out_specs=None):
@@ -399,36 +493,45 @@
     )(*args)
 
 
-def swap(axis, left, right):
+def swap(axis, first, second):
     size = lax.axis_size(axis)
-    odd = lax.axis_index(axis) % 2 == 1
     even_pairs = [(i, i ^ 1) for i in range(size)]
     odd_pairs = [(i, ((i + 1) ^ 1) - 1) for i in range(1, size - 1)]
-    first = lax.ppermute(jnp.where(odd, left, right), axis, even_pairs)
-    second = lax.ppermute(jnp.where(odd, right, left), axis, odd_pairs)
-    return jnp.where(odd, first, second), jnp.where(odd, second, first)
+    return lax.ppermute(first, axis, even_pairs), lax.ppermute(second, axis, odd_pairs)
 
 
 def body(velocity, viscosity, fibre_coords, fibre_elem, block_count, fibre_velocity):
     vel = velocity.reshape(3, 128, 512)
     visc = viscosity.reshape(128, 512)
     coords = fibre_coords.reshape(32, 4, 3, 128).transpose(0, 2, 1, 3)
-    idents = fibre_elem.reshape(32, 4)
-    counts = block_count.reshape(32, 1)
+    idents = fibre_elem.reshape(32, 4).transpose(1, 0)
+    counts = block_count.reshape(32)
     own_velocity = fibre_velocity.reshape(32, 4, 3, 128).transpose(0, 2, 1, 3)
-    live = lax.broadcasted_iota(jnp.int32, (32, 4), 1) < counts
-    (packed,) = call(pack_kernel, [(32, 13, 1, 128)], (coords, idents, counts))
+    odds = jnp.stack([lax.axis_index(axis) % 2 for axis in ("gx", "gy", "gz")]).astype(jnp.int32)
+    place = lax.axis_index("gz").astype(jnp.int32).reshape(1)
+    (packed,) = call(
+        pack_kernel, [(32, 13, 1, 128)], (coords, idents, counts.reshape(1, 32)), specs=[hbm] * 3,
+        scratch=[
+            pltpu.VMEM((32, 3, 4, 128), f32),
+            pltpu.VMEM((4, 32), jnp.int32),
+            pltpu.VMEM((1, 32), jnp.int32),
+            pltpu.SemaphoreType.DMA((3,)),
+        ],
+    )
     got = lax.all_to_all(packed, "gz", split_axis=0, concat_axis=0, tiled=True)
 
     dx, dyz, mass = operator_tables()
     field = (3, 128, 512)
     y_face, z_face = (3, 32, 128), (3, 16, 128)
-    adv, helm, xl, xr, yl, yr, zl, zr = call(
-        fluid_kernel, [field, field] + [y_face] * 4 + [z_face] * 2, (vel, visc, dx, dyz, mass),
-        specs=[hbm] * 5,
-        out_specs=[hbm] * 2 + [vmem] * 6,
+    y_pair, z_pair = (2,) + y_face, (2,) + z_face
+    adv, helm, x_sends, y_raw, z_raw, table = call(
+        fluid_kernel, [field, field, y_pair, y_pair, z_pair, (48 * 128, 128)], (odds, vel, visc, dx, dyz, mass),
+        specs=[smem] + [hbm] * 5,
+        out_specs=[hbm] * 2 + [vmem] + [hbm] * 2 + [vmem],
         scratch=[
             pltpu.VMEM((3, 384, 512), f32),
+            pltpu.VMEM(y_pair, f32),
+            pltpu.VMEM(z_pair, f32),
             pltpu.VMEM(field, f32),
             pltpu.VMEM(field, f32),
             pltpu.VMEM(field, f32),
@@ -436,38 +539,45 @@
             pltpu.VMEM(dx.shape, f32),
             pltpu.VMEM(dyz.shape, f32),
             pltpu.VMEM((1, 512), f32),
-            pltpu.SemaphoreType.DMA((11,)),
+            pltpu.SemaphoreType.DMA((14,)),
         ],
     )
-    (table,) = call(table_kernel, [(48 * 128, 128)], (vel,))
-    xb, xa = swap("gx", xl, xr)
-    yl, yr = call(y_face_kernel, [y_face] * 2, (xb, xa, yl, yr))
-    yb, ya = swap("gy", yl, yr)
-    got, yl = lax.optimization_barrier((got, yl))
+    x1, x2 = swap("gx", x_sends[0], x_sends[1])
+    got, y_raw = lax.optimization_barrier((got, y_raw))
     (values,) = call(
-        fibre_kernel, [(32, 12, 1, 128)], (got, table, basis_table(), got),
-        specs=[anywhere, vmem, vmem, vmem],
+        fibre_kernel, [(32, 12, 1, 128)], (place, got, table),
+        specs=[smem, hbm, vmem], out_specs=[hbm],
         scratch=[
+            pltpu.VMEM((32, 13, 1, 128), f32),
+            pltpu.VMEM((32, 12, 1, 128), f32),
             pltpu.SMEM((128 + 2 * UNROLL,), jnp.int32),
             pltpu.SMEM((32, 128), f32),
-            pltpu.SemaphoreType.DMA,
+            pltpu.SemaphoreType.DMA((3,)),
         ],
     )
-    values, yb, ya = lax.optimization_barrier((values, yb, ya))
-    zl, zr = call(z_face_kernel, [z_face] * 2, (xb, xa, yb, ya, zl, zr))
-    zb, za = swap("gz", zl, zr)
+    values, x1, x2 = lax.optimization_barrier((values, x1, x2))
+    sampled = lax.all_to_all(values, "gz", split_axis=0, concat_axis=0, tiled=True)
+    y1, y2, x1, x2, z_raw = call(
+        y_face_kernel, [y_face] * 4 + [z_pair], (odds, x1, x2, y_raw, z_raw), specs=[smem] + [hbm] * 4,
+        scratch=[pltpu.VMEM(y_pair, f32), pltpu.SemaphoreType.DMA((4,))],
+    )
+    y1, y2 = swap("gy", y1, y2)
+    z1, z2 = call(
+        z_face_kernel, [z_face] * 2, (odds, x1, x2, y1, y2, z_raw), specs=[smem] + [vmem] * 5,
+        scratch=[pltpu.VMEM(z_pair, f32)],
+    )
+    z1, z2 = swap("gz", z1, z2)
+    (work,) = call(
+        side_kernel, [(6, 128, 512)], (odds, adv, helm, x1, x2, y1, y2), specs=[smem, hbm, hbm] + [vmem] * 4,
+        scratch=[pltpu.SemaphoreType.DMA((6,))],
+    )
     adv, helm = call(
-        end_kernel, [field, field], (adv, helm, xb, xa, yb, ya, zb, za),
-        specs=[hbm] * 2 + [vmem] * 6, out_specs=[hbm] * 2,
-        scratch=[
-            pltpu.VMEM((6, 128, 512), f32),
-            pltpu.SemaphoreType.DMA((12,)),
-        ],
-    )
-    sampled = lax.all_to_all(values, "gz", split_axis=0, concat_axis=0, tiled=True).reshape(32, 3, 4, 128)
-    relative = sampled - own_velocity
-    factor = jnp.sqrt(1.0 + jnp.sum(relative * relative, axis=1, keepdims=True))
-    drag = jnp.where(live[:, None, :, None], drag_scale * factor * relative, 0.0)
+        end_kernel, [field, field], (odds, work, z1, z2), specs=[smem] + [vmem] * 3, out_specs=[hbm] * 2,
+        scratch=[pltpu.VMEM((6, 128, 512), f32), pltpu.SemaphoreType.DMA((6,))],
+    )
+    (drag,) = call(
+        drag_kernel, [(32, 3, 4, 128)], (counts, sampled, own_velocity), specs=[smem, vmem, vmem]
+    )
     drag = drag.transpose(0, 2, 1, 3).reshape(fibre_coords.shape)
     return adv.reshape(velocity.shape), helm.reshape(velocity.shape), drag
 

time: 87.1 us -> 76.8 us (0.88)
  the two profiles are of different devices: /device:TPU:20 before, /device:TPU:17 now
where the time goes in v2:
time: 76.8 us; the launch traced here: 76.2 us
  starting transfers between devices  42.1 us (55%)
  Pallas kernels  25.2 us (33%)
  waiting for transfers between devices  7.25 us (9%)
  between operations  0.87 us (1%)
    pallas_call x8, Pallas kernels, call(): pl.pallas_call(kernel, out_shape=shapes, in_specs=specs or [vmem] * len(a...  25.2 us
    all_to_all x1, starting transfers between devices, body(): got = lax.all_to_all(packed, 'gz', split_axis=0, concat_axis=0, tiled=True)  15.9 us
    ppermute x3, starting transfers between devices, swap(): lax.ppermute(first, axis, even_pairs)  11.4 us
    all_to_all x1, starting transfers between devices, body(): lax.all_to_all(values, 'gz', split_axis=0, concat_axis=0, tiled=True)  8.89 us
    ppermute x3, starting transfers between devices, swap(): lax.ppermute(second, axis, odd_pairs)  5.9 us
    all_to_all x1, waiting for transfers between devices, body(): got = lax.all_to_all(packed, 'gz', split_axis=0, concat_axis=0, tiled=True)  4.04 us
    ppermute x3, waiting for transfers between devices, swap(): lax.ppermute(second, axis, odd_pairs)  2.55 us
  transfers between devices with their start and end apart: 8, of which 3 were waited for; matrix products, arithmetic and copies ran while one was open for 0% of the time, Pallas kernels for 29%

profile of v2, /device:TPU:17, one launch (start us, length us, event | category | flops | bytes accessed | tf_op | source)
XLA Modules:
  0.0 76.2 jit_solution(272507931374999254)
XLA Ops:
  0.6 1.8 %pack_kernel.1 = f32[32,13,1,128]{3,2,1,0:T(1,128)} custom-call(f32[32,3,4,128]{3,2,1,0:T(4,128)} %bitcast.31, s32[4,32]{1,0:T(4,128)} %bitcast.33, s32[1,32]{1,0:T(1,128)} %bitcast.27), custom_call_target="tpu_custom_call" | custom-call | tf_op jit(solution)/shard_map/pack_kernel/pallas_call | solution.py:485
  2.4 15.9 %all-to-all-start = ((f32[32,13,1,128]{3,2,1,0:T(1,128)}), f32[32,13,1,128]{3,2,1,0:T(1,128)S(1)}, u32[]{:S(2)}, u32[]{:S(2)}) async-start(f32[32,13,1,128]{3,2,1,0:T(1,128)} %pack_kernel.1), calls=%async_computation | async-start | bytes 425984 | tf_op jit(solution)/shard_map/all_to_all | solution.py:521
  18.4 0.1 pad_add_fusion.odds
  18.5 9.0 %fluid_kernel.1 = (f32[3,128,512]{2,1,0:T(8,128)}, f32[3,128,512]{2,1,0:T(8,128)}, f32[2,3,32,128]{3,2,1,0:T(8,128)S(1)}, f32[2,3,32,128]{3,2,1,0:T(8,128)}, f32...) custom-call(s32[3]{0:T(128)S(1)} %pad_add_fusion.odds, f32[3,128,512]{2,1,0:T(8,128)} %bitcast.29, f32[128,512]{1,0:T(8,128)} %bitcast.30, ...), custom_call_target="tpu_custom_call" | custom-call | tf_op jit(solution)/shard_map/fluid_kernel/pallas_call | solution.py:485
  27.5 0.7 collective-permute-start.1
  28.2 5.6 %collective-permute-start = (f32[3,32,128]{2,1,0:T(8,128)S(1)}, f32[3,32,128]{2,1,0:T(8,128)}, u32[]{:S(2)}, u32[]{:S(2)}) collective-permute-start(f32[3,32,128]{2,1,0:T(8,128)S(1)} %get-tuple-element.44), channel_id=1, source_target_pairs={{0,128},{128,0},{256,384},{384,256},{1,129},{129,1},{257,385},{385... | collective-permute-start | bytes 147464 | tf_op jit(solution)/shard_map/ppermute | solution.py:500
  33.8 4.0 %all-to-all-done.got_in = f32[32,13,1,128]{3,2,1,0:T(1,128)S(1)} async-done(((f32[32,13,1,128]{3,2,1,0:T(1,128)}), f32[32,13,1,128]{3,2,1,0:T(1,128)S(1)}, u32[]{:S(2)}, u32[]{:S(2)}) %all-to-all-start) | async-done | bytes 213024 | tf_op jit(solution)/shard_map/all_to_all | solution.py:521
  37.8 0.0 copy-start.2
  37.8 0.7 copy-done.2
  38.5 6.0 %fibre_kernel.1 = f32[32,12,1,128]{3,2,1,0:T(1,128)} custom-call(s32[1]{0:T(128)} %bitcast.5.place, f32[32,13,1,128]{3,2,1,0:T(1,128)} %copy-done.2, f32[6144,128]{1,0:T(8,128)S(1)} %get-tuple-element.27.table), custom_call_target="tpu_custom_call" | custom-call | tf_op jit(solution)/shard_map/fibre_kernel/pallas_call | solution.py:485
  44.5 0.0 copy-start
  44.5 0.0 copy-start.1
  44.5 0.0 collective-permute-done.1.x2_in
  44.5 0.0 copy-start.3
  44.5 0.0 collective-permute-done.x1_in
  44.5 8.9 %all-to-all-start.1 = ((f32[32,12,1,128]{3,2,1,0:T(1,128)}), f32[32,12,1,128]{3,2,1,0:T(1,128)S(1)}, u32[]{:S(2)}, u32[]{:S(2)}) async-start(f32[32,12,1,128]{3,2,1,0:T(1,128)} %fibre_kernel.1), calls=%async_computation.1 | async-start | bytes 393216 | tf_op jit(solution)/shard_map/all_to_all | solution.py:559
  53.4 0.0 copy-done.3
  53.4 1.6 %y_face_kernel.1 = (f32[3,32,128]{2,1,0:T(8,128)S(1)}, f32[3,32,128]{2,1,0:T(8,128)S(1)}, f32[3,32,128]{2,1,0:T(8,128)S(1)}, f32[3,32,128]{2,1,0:T(8,128)S(1)}, f32[2,3,16,128]{3,2,1,0:T(8,128)S(1)}) custom-call(s32[3]{0:T(128)S(1)} %pad_add_fusion.odds, f32[3,32,128]{2,1,0:T(8,128)} %collective-permute-done.x1_in, f32[3,32,128]{2,1,0:T(8,128)} %copy-done.3, ...), custom_call_target="tpu_custom_call" | custom-call | tf_op jit(solution)/shard_map/y_face_kernel/pallas_call | solution.py:485
  55.0 2.5 %collective-permute-start.2 = (f32[3,32,128]{2,1,0:T(8,128)S(1)}, f32[3,32,128]{2,1,0:T(8,128)S(1)}, u32[]{:S(2)}, u32[]{:S(2)}) collective-permute-start(f32[3,32,128]{2,1,0:T(8,128)S(1)} %get-tuple-element.35), channel_id=1, source_target_pairs={{0,32},{32,0},{64,96},{96,64},{1,33},{33,1},{65,97},{97,65},{2,34}... | collective-permute-start | bytes 147464 | tf_op jit(solution)/shard_map/ppermute | solution.py:500
  57.6 1.9 %collective-permute-start.3 = (f32[3,32,128]{2,1,0:T(8,128)S(1)}, f32[3,32,128]{2,1,0:T(8,128)S(1)}, u32[]{:S(2)}, u32[]{:S(2)}) collective-permute-start(f32[3,32,128]{2,1,0:T(8,128)S(1)} %get-tuple-element.36), channel_id=1, source_target_pairs={{32,64},{64,32},{33,65},{65,33},{34,66},{66,34},{35,67},{67,35},{3... | collective-permute-start | bytes 147464 | tf_op jit(solution)/shard_map/ppermute | solution.py:500
  59.5 0.7 collective-permute-done.2.y1
  60.2 2.5 %collective-permute-done.3.y2 = f32[3,32,128]{2,1,0:T(8,128)S(1)} collective-permute-done((f32[3,32,128]{2,1,0:T(8,128)S(1)}, f32[3,32,128]{2,1,0:T(8,128)S(1)}, u32[]{:S(2)}, u32[]{:S(2)}) %collective-permute-start.3) | collective-permute-done | bytes 49184 | tf_op jit(solution)/shard_map/ppermute | solution.py:500
  62.7 0.8 %z_face_kernel.1 = (f32[3,16,128]{2,1,0:T(8,128)S(1)}, f32[3,16,128]{2,1,0:T(8,128)S(1)}) custom-call(s32[3]{0:T(128)S(1)} %pad_add_fusion.odds, f32[3,32,128]{2,1,0:T(8,128)S(1)} %get-tuple-element.33.x1, f32[3,32,128]{2,1,0:T(8,128)S(1)} %get-tuple-element.34.x2, f32[3,32,128]{2,1,0:T(8,128)S(1)} %collective-permute-done.2.y1, ...), custom_call_target="tpu_custom_call" | custom-call | tf_op jit(solution)/shard_map/z_face_kernel/pallas_call | solution.py:485
  63.5 3.3 %collective-permute-start.4 = (f32[3,16,128]{2,1,0:T(8,128)S(1)}, f32[3,16,128]{2,1,0:T(8,128)S(1)}, u32[]{:S(2)}, u32[]{:S(2)}) collective-permute-start(f32[3,16,128]{2,1,0:T(8,128)S(1)} %get-tuple-element.38), channel_id=1, source_target_pairs={{0,1},{1,0},{2,3},{3,2},{4,5},{5,4},{6,7},{7,6},{8,9},{9,8},{10,11... | collective-permute-start | bytes 73736 | tf_op jit(solution)/shard_map/ppermute | solution.py:500
  66.8 3.3 %collective-permute-start.5 = (f32[3,16,128]{2,1,0:T(8,128)S(1)}, f32[3,16,128]{2,1,0:T(8,128)S(1)}, u32[]{:S(2)}, u32[]{:S(2)}) collective-permute-start(f32[3,16,128]{2,1,0:T(8,128)S(1)} %get-tuple-element.39), channel_id=1, source_target_pairs={{1,2},{2,1},{3,4},{4,3},{5,6},{6,5},{7,8},{8,7},{9,10},{10,9},{11,... | collective-permute-start | bytes 73736 | tf_op jit(solution)/shard_map/ppermute | solution.py:500
  70.1 2.4 %side_kernel.1.work = f32[6,128,512]{2,1,0:T(8,128)S(1)} custom-call(s32[3]{0:T(128)S(1)} %pad_add_fusion.odds, f32[3,128,512]{2,1,0:T(8,128)} %get-tuple-element.23.adv_in, f32[3,128,512]{2,1,0:T(8,128)} %get-tuple-element.24.helm_in, f32[3,32,128]{2,1,0:T(8,128)S(1)} %get-tuple-element.33.x1, f32[3,32,128]{2,1,0:T(8,128)S(1)} %get-tuple-element.34.x2, ...), custom_call_target="tpu_custom_call" | custom-call | tf_op jit(solution)/shard_map/side_kernel/pallas_call | solution.py:485
  72.5 0.0 collective-permute-done.4.z1
  72.6 0.0 collective-permute-done.5.z2
  72.6 2.2 %end_kernel.1 = (f32[3,128,512]{2,1,0:T(8,128)}, f32[3,128,512]{2,1,0:T(8,128)}) custom-call(s32[3]{0:T(128)S(1)} %pad_add_fusion.odds, f32[6,128,512]{2,1,0:T(8,128)S(1)} %side_kernel.1.work, f32[3,16,128]{2,1,0:T(8,128)S(1)} %collective-permute-done.4.z1, f32[3,16,128]{2,1,0:T(8,128)S(1)} %collective-permute-done.5.z2), custom_call_target="tpu_custom_call" | custom-call | tf_op jit(solution)/shard_map/end_kernel/pallas_call | solution.py:485
  74.8 0.0 all-to-all-done.1.sampled
  74.8 0.0 copy-done
  74.8 0.0 copy-done.1
  74.8 1.4 %drag_kernel.1 = f32[32,3,4,128]{3,2,1,0:T(4,128)} custom-call(s32[32]{0:T(128)S(1)} %bitcast.28, f32[32,12,1,128]{3,2,1,0:T(1,128)S(1)} %all-to-all-done.1.sampled, f32[32,3,4,128]{3,2,1,0:T(4,128)S(1)} %bitcast.26), custom_call_target="tpu_custom_call" | custom-call | tf_op jit(solution)/shard_map/drag_kernel/pallas_call | solution.py:485
  (1 shorter events, 0.0 us)
Async XLA Ops:
  2.4 35.4 %all-to-all-start = ((f32[32,13,1,128]{3,2,1,0:T(1,128)}), f32[32,13,1,128]{3,2,1,0:T(1,128)S(1)}, u32[]{:S(2)}, u32[]{:S(2)}) async-start(f32[32,13,1,128]{3,2,1,0:T(1,128)} %pack_kernel.1), calls=%async_computation | async-start | bytes 425984 | tf_op jit(solution)/shard_map/all_to_all | solution.py:521
  27.5 17.0 %collective-permute-start.1 = (f32[3,32,128]{2,1,0:T(8,128)S(1)}, f32[3,32,128]{2,1,0:T(8,128)S(1)}, u32[]{:S(2)}, u32[]{:S(2)}) collective-permute-start(f32[3,32,128]{2,1,0:T(8,128)S(1)} %get-tuple-element.43), channel_id=1, source_target_pairs={{128,256},{256,128},{129,257},{257,129},{130,258},{258,130},{131,2... | collective-permute-start | bytes 147464 | tf_op jit(solution)/shard_map/ppermute | solution.py:500
  28.2 16.3 %collective-permute-start = (f32[3,32,128]{2,1,0:T(8,128)S(1)}, f32[3,32,128]{2,1,0:T(8,128)}, u32[]{:S(2)}, u32[]{:S(2)}) collective-permute-start(f32[3,32,128]{2,1,0:T(8,128)S(1)} %get-tuple-element.44), channel_id=1, source_target_pairs={{0,128},{128,0},{256,384},{384,256},{1,129},{129,1},{257,385},{385... | collective-permute-start | bytes 147464 | tf_op jit(solution)/shard_map/ppermute | solution.py:500
  37.8 0.7 copy-start.2
  44.5 30.4 %copy-start = (f32[1,1,1,32,4,3,128]{6,4,5,3,2,1,0:T(4,128)S(1)}, f32[1,1,1,32,4,3,128]{6,4,5,3,2,1,0:T(4,128)}, u32[]{:S(2)}) copy-start(f32[1,1,1,32,4,3,128]{6,4,5,3,2,1,0:T(4,128)} %param.14) | copy-start | bytes 589828
  44.5 30.3 %copy-start.1 = (s32[1,1,1,32]{3,2,1,0:T(1,128)S(1)}, s32[1,1,1,32]{3,2,1,0:T(1,128)}, u32[]{:S(2)}) copy-start(s32[1,1,1,32]{3,2,1,0:T(1,128)} %param.13) | copy-start | bytes 388
  44.5 8.9 %copy-start.3 = (f32[3,32,128]{2,1,0:T(8,128)}, f32[3,32,128]{2,1,0:T(8,128)S(1)}, u32[]{:S(2)}) copy-start(f32[3,32,128]{2,1,0:T(8,128)S(1)} %collective-permute-done.1.x2_in) | copy-start | bytes 147460
  44.5 30.3 %all-to-all-start.1 = ((f32[32,12,1,128]{3,2,1,0:T(1,128)}), f32[32,12,1,128]{3,2,1,0:T(1,128)S(1)}, u32[]{:S(2)}, u32[]{:S(2)}) async-start(f32[32,12,1,128]{3,2,1,0:T(1,128)} %fibre_kernel.1), calls=%async_computation.1 | async-start | bytes 393216 | tf_op jit(solution)/shard_map/all_to_all | solution.py:559
  55.0 5.1 %collective-permute-start.2 = (f32[3,32,128]{2,1,0:T(8,128)S(1)}, f32[3,32,128]{2,1,0:T(8,128)S(1)}, u32[]{:S(2)}, u32[]{:S(2)}) collective-permute-start(f32[3,32,128]{2,1,0:T(8,128)S(1)} %get-tuple-element.35), channel_id=1, source_target_pairs={{0,32},{32,0},{64,96},{96,64},{1,33},{33,1},{65,97},{97,65},{2,34}... | collective-permute-start | bytes 147464 | tf_op jit(solution)/shard_map/ppermute | solution.py:500
  57.6 5.1 %collective-permute-start.3 = (f32[3,32,128]{2,1,0:T(8,128)S(1)}, f32[3,32,128]{2,1,0:T(8,128)S(1)}, u32[]{:S(2)}, u32[]{:S(2)}) collective-permute-start(f32[3,32,128]{2,1,0:T(8,128)S(1)} %get-tuple-element.36), channel_id=1, source_target_pairs={{32,64},{64,32},{33,65},{65,33},{34,66},{66,34},{35,67},{67,35},{3... | collective-permute-start | bytes 147464 | tf_op jit(solution)/shard_map/ppermute | solution.py:500
  63.5 9.0 %collective-permute-start.4 = (f32[3,16,128]{2,1,0:T(8,128)S(1)}, f32[3,16,128]{2,1,0:T(8,128)S(1)}, u32[]{:S(2)}, u32[]{:S(2)}) collective-permute-start(f32[3,16,128]{2,1,0:T(8,128)S(1)} %get-tuple-element.38), channel_id=1, source_target_pairs={{0,1},{1,0},{2,3},{3,2},{4,5},{5,4},{6,7},{7,6},{8,9},{9,8},{10,11... | collective-permute-start | bytes 73736 | tf_op jit(solution)/shard_map/ppermute | solution.py:500
  66.8 5.8 %collective-permute-start.5 = (f32[3,16,128]{2,1,0:T(8,128)S(1)}, f32[3,16,128]{2,1,0:T(8,128)S(1)}, u32[]{:S(2)}, u32[]{:S(2)}) collective-permute-start(f32[3,16,128]{2,1,0:T(8,128)S(1)} %get-tuple-element.39), channel_id=1, source_target_pairs={{1,2},{2,1},{3,4},{4,3},{5,6},{6,5},{7,8},{8,7},{9,10},{10,9},{11,... | collective-permute-start | bytes 73736 | tf_op jit(solution)/shard_map/ppermute | solution.py:500

commit v3 on v2

--- a/solution.py
+++ b/solution.py
@@ -53,20 +53,44 @@
     return derivative
 
 
-def operator_tables():
+def operator_rows():
     derivative = derivative_table()
-    identity = np.eye(8)
-    kron_x = np.kron(np.kron(derivative, identity), identity)
-    kron_y = np.kron(np.eye(4), np.kron(derivative, identity))
-    kron_z = np.kron(np.eye(32), derivative)
-    kron_yz = np.concatenate([kron_y, kron_z], 0)
+    lanes = np.arange(128)
+    along_x = np.zeros((8, 4, 128))
+    for half in range(2):
+        along_x[:, :, 64 * half : 64 * half + 64] = derivative[:, half::2, None]
+    along_y = derivative[:, lanes // 8 % 8]
+    along_z = derivative[:, lanes % 8]
+    rows = np.concatenate([along_x.reshape(32, 128), along_y, along_z]).astype(np.float32)
     weights = np.asarray(gll_weights)
-    mass = (weights[:, None, None] * weights[None, :, None] * weights[None, None, :]).reshape(1, 512)
-    return (
-        kron_x.astype(np.float32),
-        kron_yz.astype(np.float32),
-        mass.astype(np.float32),
-    )
+    mass = (weights[:, None, None] * weights[None, :, None] * weights[None, None, :]).reshape(4, 128)
+    mass = np.concatenate([mass, np.zeros((4, 128))]).astype(np.float32)
+    return np.concatenate([rows, mass])
+
+
+def fill_operators(rows, dx, dyz):
+    row = lax.broadcasted_iota(jnp.int32, (64, 128), 0)
+    lane = lax.broadcasted_iota(jnp.int32, (64, 128), 1)
+    same = (row & 63) == (lane & 63)
+    for a in range(8):
+        for tile in range(4):
+            values = jnp.where(same, rows[4 * a + tile : 4 * a + tile + 1], 0.0)
+            high, low = split(values)
+            dx[0, 64 * a : 64 * a + 64, 128 * tile : 128 * tile + 128] = high
+            dx[1, 64 * a : 64 * a + 64, 128 * tile : 128 * tile + 128] = low
+    row = lax.broadcasted_iota(jnp.int32, (128, 128), 0)
+    lane = lax.broadcasted_iota(jnp.int32, (128, 128), 1)
+    along_y = jnp.concatenate([jnp.broadcast_to(rows[32 + j % 8 : 33 + j % 8], (8, 128)) for j in range(16)], 0)
+    along_z = jnp.concatenate([rows[40:48]] * 16, 0)
+    along_y = jnp.where(((row ^ lane) & 71) == 0, along_y, 0.0)
+    along_z = jnp.where((row >> 3) == (lane >> 3), along_z, 0.0)
+    empty = jnp.zeros((128, 128), bf16)
+    for start, values in ((0, along_y), (256, along_z)):
+        for n, part in enumerate(split(values)):
+            dyz[n, start : start + 128, 0:128] = part
+            dyz[n, start : start + 128, 128:256] = empty
+            dyz[n, start + 128 : start + 256, 0:128] = empty
+            dyz[n, start + 128 : start + 256, 128:256] = part
 
 
 def pick_table(face):
@@ -138,27 +162,23 @@
     return lax.broadcasted_iota(jnp.int32, shape, len(shape) - 1)
 
 
-def fluid_kernel(odds, vel_in, visc_in, dx_in, dyz_in, mass_in, adv_out, helm_out, x_work, y_out, z_out, table, flux, y_work, z_work, adv, helm, vel, visc, dx_ref, dyz_ref, mass_ref, sems):
-    pairs = ((vel_in, vel), (dx_in, dx_ref), (dyz_in, dyz_ref), (visc_in, visc), (mass_in, mass_ref))
+def fluid_kernel(vel_in, visc_in, rows_in, adv_out, helm_out, x_work, y_out, z_out, table, flux, y_work, z_work, adv, helm, vel, visc, rows, dx, dyz, sems):
+    pairs = ((rows_in, rows), (vel_in, vel), (visc_in, visc))
     loads = [pltpu.make_async_copy(a, b, sems.at[n]) for n, (a, b) in enumerate(pairs)]
     for load in loads:
         load.start()
     loads[0].wait()
-    fill_table(vel, table, (0, 1))
+    fill_operators(rows, dx, dyz)
     loads[1].wait()
     v = vel[...].reshape(384, 512)
-    dx = split(dx_ref[...])
     flux[0] = dot3(v, dx, 1)
-    loads[2].wait()
-    dyz = split(dyz_ref[...])
     for half in range(2):
         lanes = slice(256 * half, 256 * half + 256)
         g = dot3(v[:, lanes], dyz, 1)
         flux[1, :, lanes] = g[:, :256]
         flux[2, :, lanes] = g[:, 256:]
-    loads[3].wait()
-    loads[4].wait()
-    mass = mass_ref[...]
+    loads[2].wait()
+    mass = jnp.concatenate([rows[48 + tile : 49 + tile] for tile in range(4)], 1)
     weighted = mass * visc[...]
     for c in range(3):
         rows = slice(128 * c, 128 * c + 128)
@@ -179,7 +199,7 @@
             stores.append(pltpu.make_async_copy(field.at[c], out.at[c], sems.at[5 + len(stores)]))
             stores[-1].start()
     lane = lane_iota((32, 128))
-    odd = odds[0]
+    odd = lax.axis_index("gx") % 2
     for c in range(3):
         left = jnp.where(lane < 64, adv[c, 0:32, 0:128], pltpu.roll(helm[c, 0:32, 0:128], 64, 1))
         right = jnp.where(lane < 64, pltpu.roll(adv[c, 96:128, 384:512], 64, 1), helm[c, 96:128, 384:512])
@@ -201,7 +221,7 @@
     stores[-1].start()
     stores.append(pltpu.make_async_copy(z_work, z_out, sems.at[13]))
     stores[-1].start()
-    fill_table(vel, table, (2, 3))
+    fill_table(vel, table, range(4))
     for store in stores:
         store.wait()
 
@@ -246,7 +266,7 @@
     return below, above
 
 
-def y_face_kernel(odds, x1_in, x2_in, y_in, z_in, y1, y2, x1, x2, z, y_raw, sems):
+def y_face_kernel(x1_in, x2_in, y_in, z_in, y1, y2, x1, x2, z, y_raw, sems):
     pairs = ((x1_in, x1), (x2_in, x2), (y_in, y_raw), (z_in, z))
     loads = [pltpu.make_async_copy(a, b, sems.at[n]) for n, (a, b) in enumerate(pairs)]
     for load in loads:
@@ -254,8 +274,8 @@
     for load in loads:
         load.wait()
     lane = lane_iota((8, 128)) % 64
-    xb, xa = both_sides(odds[0], x1, x2)
-    odd = jnp.full((8, 128), odds[1], jnp.int32) == 1
+    xb, xa = both_sides(lax.axis_index("gx") % 2, x1, x2)
+    odd = jnp.full((8, 128), lax.axis_index("gy") % 2, jnp.int32) == 1
     head, tail = slice(0, 8), slice(24, 32)
     for c in range(3):
         extra = {
@@ -274,13 +294,13 @@
             y2[c, rows] = jnp.where(odd, right, left)
 
 
-def z_face_kernel(odds, x1, x2, y1, y2, z_raw, out1, out2, z):
+def z_face_kernel(x1, x2, y1, y2, z_raw, out1, out2, z):
     z[...] = z_raw[...]
     lane = lane_iota((1, 128)) % 8
-    x_odd = jnp.full((96, 128), odds[0], jnp.int32) == 1
+    x_odd = jnp.full((96, 128), lax.axis_index("gx") % 2, jnp.int32) == 1
     x_first, x_second = x1[...].reshape(96, 128), x2[...].reshape(96, 128)
     xb, xa = jnp.where(x_odd, x_first, x_second), jnp.where(x_odd, x_second, x_first)
-    yb, ya = both_sides(odds[1], y1, y2)
+    yb, ya = both_sides(lax.axis_index("gy") % 2, y1, y2)
     for level, side in ((0, 0), (7, 1)):
         for got, place in ((xb, 0), (xa, 1)):
             part = pick(got, edge_table(side, place))
@@ -299,7 +319,7 @@
                     above = pltpu.roll(above, 7, 1)
                 z[side, c, 4 * a : 4 * a + 1] += jnp.where(lane == 0, below, 0.0)
                 z[side, c, 4 * a + 3 : 4 * a + 4] += jnp.where(lane == 7, above, 0.0)
-    odd = jnp.full((3, 16, 128), odds[2], jnp.int32) == 1
+    odd = jnp.full((3, 16, 128), lax.axis_index("gz") % 2, jnp.int32) == 1
     out1[...] = jnp.where(odd, z[0], z[1])
     out2[...] = jnp.where(odd, z[1], z[0])
 
@@ -312,7 +332,7 @@
     return [[got, pltpu.roll(got, 64, 1)] for got in (below, above)]
 
 
-def side_kernel(odds, adv_in, helm_in, x1, x2, y1, y2, work, sems):
+def side_kernel(adv_in, helm_in, x1, x2, y1, y2, work, sems):
     loads = []
     for c in range(3):
         for part, source in enumerate((adv_in, helm_in)):
@@ -320,8 +340,8 @@
             loads.append(pltpu.make_async_copy(source.at[c], work.at[n], sems.at[n]))
             loads[-1].start()
     lane = lane_iota((32, 128))
-    x_sides = sides(odds[0], x1, x2)
-    y_sides = sides(odds[1], y1, y2)
+    x_sides = sides(lax.axis_index("gx") % 2, x1, x2)
+    y_sides = sides(lax.axis_index("gy") % 2, y1, y2)
     wide = [[spread(y_sides[side][part], pick_table(side)) for side in range(2)] for part in range(2)]
     for load in loads:
         load.wait()
@@ -338,9 +358,9 @@
                     work[n, row : row + 8] += wide[part][side][source : source + 8]
 
 
-def end_kernel(odds, work, z1, z2, adv, helm, done, sems):
+def end_kernel(work, z1, z2, adv, helm, done, sems):
     level = lax.broadcasted_iota(jnp.int32, (16, 8, 512), 1)
-    z_sides = sides(odds[2], z1, z2)
+    z_sides = sides(lax.axis_index("gz") % 2, z1, z2)
     stores = []
     for part, target in enumerate((adv, helm)):
         ends = [spread(z_sides[side][part], pick_table(2 + side)) for side in range(2)]
@@ -401,13 +421,11 @@
                 table[128 * row : 128 * row + 128] = mixed
 
 
-def fibre_kernel(place, got_in, table, out_hbm, got, out, live, tags, sems):
-    load_tags = pltpu.make_async_copy(got_in.at[:, 12, 0], tags, sems.at[0])
+def fibre_kernel(got, table, out_hbm, out, live, tags, sems):
+    load_tags = pltpu.make_async_copy(got.at[:, 12, 0], tags, sems.at[0])
     load_tags.start()
-    load_got = pltpu.make_async_copy(got_in, got, sems.at[1])
-    load_got.start()
     load_tags.wait()
-    me = place[0]
+    me = lax.axis_index("gz")
 
     def ids(block):
         return tags[block // 4, block % 4 * 32 + me]
@@ -421,7 +439,6 @@
 
     count = lax.fori_loop(0, 128, gather, 0, unroll=8)
     live[count] = 0
-    load_got.wait()
     rows, scales = basis_rows()
 
     def weights(position):
@@ -462,7 +479,7 @@
         return carry
 
     lax.fori_loop(0, (count + UNROLL - 1) // UNROLL, group, 0)
-    store = pltpu.make_async_copy(out, out_hbm, sems.at[2])
+    store = pltpu.make_async_copy(out, out_hbm, sems.at[1])
     store.start()
     store.wait()
 
@@ -507,8 +524,6 @@
     idents = fibre_elem.reshape(32, 4).transpose(1, 0)
     counts = block_count.reshape(32)
     own_velocity = fibre_velocity.reshape(32, 4, 3, 128).transpose(0, 2, 1, 3)
-    odds = jnp.stack([lax.axis_index(axis) % 2 for axis in ("gx", "gy", "gz")]).astype(jnp.int32)
-    place = lax.axis_index("gz").astype(jnp.int32).reshape(1)
     (packed,) = call(
         pack_kernel, [(32, 13, 1, 128)], (coords, idents, counts.reshape(1, 32)), specs=[hbm] * 3,
         scratch=[
@@ -520,13 +535,13 @@
     )
     got = lax.all_to_all(packed, "gz", split_axis=0, concat_axis=0, tiled=True)
 
-    dx, dyz, mass = operator_tables()
+    rows = operator_rows()
     field = (3, 128, 512)
     y_face, z_face = (3, 32, 128), (3, 16, 128)
     y_pair, z_pair = (2,) + y_face, (2,) + z_face
     adv, helm, x_sends, y_raw, z_raw, table = call(
-        fluid_kernel, [field, field, y_pair, y_pair, z_pair, (48 * 128, 128)], (odds, vel, visc, dx, dyz, mass),
-        specs=[smem] + [hbm] * 5,
+        fluid_kernel, [field, field, y_pair, y_pair, z_pair, (48 * 128, 128)], (vel, visc, rows),
+        specs=[hbm] * 3,
         out_specs=[hbm] * 2 + [vmem] + [hbm] * 2 + [vmem],
         scratch=[
             pltpu.VMEM((3, 384, 512), f32),
@@ -536,43 +551,42 @@
             pltpu.VMEM(field, f32),
             pltpu.VMEM(field, f32),
             pltpu.VMEM((128, 512), f32),
-            pltpu.VMEM(dx.shape, f32),
-            pltpu.VMEM(dyz.shape, f32),
-            pltpu.VMEM((1, 512), f32),
+            pltpu.VMEM((56, 128), f32),
+            pltpu.VMEM((2, 512, 512), bf16),
+            pltpu.VMEM((2, 512, 256), bf16),
             pltpu.SemaphoreType.DMA((14,)),
         ],
     )
     x1, x2 = swap("gx", x_sends[0], x_sends[1])
     got, y_raw = lax.optimization_barrier((got, y_raw))
     (values,) = call(
-        fibre_kernel, [(32, 12, 1, 128)], (place, got, table),
-        specs=[smem, hbm, vmem], out_specs=[hbm],
+        fibre_kernel, [(32, 12, 1, 128)], (got, table),
+        specs=[vmem, vmem], out_specs=[hbm],
         scratch=[
-            pltpu.VMEM((32, 13, 1, 128), f32),
             pltpu.VMEM((32, 12, 1, 128), f32),
             pltpu.SMEM((128 + 2 * UNROLL,), jnp.int32),
             pltpu.SMEM((32, 128), f32),
-            pltpu.SemaphoreType.DMA((3,)),
+            pltpu.SemaphoreType.DMA((2,)),
         ],
     )
     values, x1, x2 = lax.optimization_barrier((values, x1, x2))
     sampled = lax.all_to_all(values, "gz", split_axis=0, concat_axis=0, tiled=True)
     y1, y2, x1, x2, z_raw = call(
-        y_face_kernel, [y_face] * 4 + [z_pair], (odds, x1, x2, y_raw, z_raw), specs=[smem] + [hbm] * 4,
+        y_face_kernel, [y_face] * 4 + [z_pair], (x1, x2, y_raw, z_raw), specs=[hbm] * 4,
         scratch=[pltpu.VMEM(y_pair, f32), pltpu.SemaphoreType.DMA((4,))],
     )
     y1, y2 = swap("gy", y1, y2)
     z1, z2 = call(
-        z_face_kernel, [z_face] * 2, (odds, x1, x2, y1, y2, z_raw), specs=[smem] + [vmem] * 5,
+        z_face_kernel, [z_face] * 2, (x1, x2, y1, y2, z_raw), specs=[vmem] * 5,
         scratch=[pltpu.VMEM(z_pair, f32)],
     )
     z1, z2 = swap("gz", z1, z2)
     (work,) = call(
-        side_kernel, [(6, 128, 512)], (odds, adv, helm, x1, x2, y1, y2), specs=[smem, hbm, hbm] + [vmem] * 4,
+        side_kernel, [(6, 128, 512)], (adv, helm, x1, x2, y1, y2), specs=[hbm, hbm] + [vmem] * 4,
         scratch=[pltpu.SemaphoreType.DMA((6,))],
     )
     adv, helm = call(
-        end_kernel, [field, field], (odds, work, z1, z2), specs=[smem] + [vmem] * 3, out_specs=[hbm] * 2,
+        end_kernel, [field, field], (work, z1, z2), specs=[vmem] * 3, out_specs=[hbm] * 2,
         scratch=[pltpu.VMEM((6, 128, 512), f32), pltpu.SemaphoreType.DMA((6,))],
     )
     (drag,) = call(

time: 76.8 us -> 73.3 us (0.954)
  Pallas kernels: 25.2 us -> 22 us
  waiting for transfers between devices: 7.25 us -> 8.52 us
    pallas_call x8, Pallas kernels: 25.2 us -> 22 us  [call(): pl.pallas_call(kernel, out_shape=shapes, in_specs=specs or [vmem] * len(a...]
    all_to_all x1, starting transfers between devices: 8.89 us -> 7.05 us  [body(): lax.all_to_all(values, 'gz', split_axis=0, concat_axis=0, tiled=True)]
    ppermute x3, starting transfers between devices: 11.4 us -> 12.5 us  [swap(): lax.ppermute(first, axis, even_pairs)]
    all_to_all x1, waiting for transfers between devices: 4.04 us -> 5.1 us  [body(): got = lax.all_to_all(packed, 'gz', split_axis=0, concat_axis=0, tiled=True)]
    ppermute x3, waiting for transfers between devices: 2.55 us -> 3.39 us  [swap(): lax.ppermute(second, axis, odd_pairs)]
  transfers between devices with their start and end apart: 8 -> 8, of which waited for: 3 -> 3; matrix products, arithmetic and copies ran while one was open for 0% -> 0% of each run, Pallas kernels for 29% -> 26%
where the time goes in v3:
time: 73.3 us; the launch traced here: 72.8 us
  starting transfers between devices  41.4 us (56%)
  Pallas kernels  22 us (30%)
  waiting for transfers between devices  8.52 us (12%)
  between operations  0.85 us (1%)
    pallas_call x8, Pallas kernels, call(): pl.pallas_call(kernel, out_shape=shapes, in_specs=specs or [vmem] * len(a...  22 us
    all_to_all x1, starting transfers between devices, body(): got = lax.all_to_all(packed, 'gz', split_axis=0, concat_axis=0, tiled=True)  15.9 us
    ppermute x3, starting transfers between devices, swap(): lax.ppermute(first, axis, even_pairs)  12.5 us
    all_to_all x1, starting transfers between devices, body(): lax.all_to_all(values, 'gz', split_axis=0, concat_axis=0, tiled=True)  7.05 us
    ppermute x3, starting transfers between devices, swap(): lax.ppermute(second, axis, odd_pairs)  5.91 us
    all_to_all x1, waiting for transfers between devices, body(): got = lax.all_to_all(packed, 'gz', split_axis=0, concat_axis=0, tiled=True)  5.1 us
    ppermute x3, waiting for transfers between devices, swap(): lax.ppermute(second, axis, odd_pairs)  3.39 us
  transfers between devices with their start and end apart: 8, of which 3 were waited for; matrix products, arithmetic and copies ran while one was open for 0% of the time, Pallas kernels for 26%

profile of v3, /device:TPU:17, one launch (start us, length us, event | category | flops | bytes accessed | tf_op | source)
XLA Modules:
  0.0 72.8 jit_solution(16549917966947055069)
XLA Ops:
  0.6 1.8 %pack_kernel.1 = f32[32,13,1,128]{3,2,1,0:T(1,128)} custom-call(f32[32,3,4,128]{3,2,1,0:T(4,128)} %bitcast.27, s32[4,32]{1,0:T(4,128)} %bitcast.29, s32[1,32]{1,0:T(1,128)} %bitcast.23), custom_call_target="tpu_custom_call" | custom-call | tf_op jit(solution)/shard_map/pack_kernel/pallas_call | solution.py:502
  2.4 15.9 %all-to-all-start = ((f32[32,13,1,128]{3,2,1,0:T(1,128)}), f32[32,13,1,128]{3,2,1,0:T(1,128)S(1)}, u32[]{:S(2)}, u32[]{:S(2)}) async-start(f32[32,13,1,128]{3,2,1,0:T(1,128)} %pack_kernel.1), calls=%async_computation | async-start | bytes 425984 | tf_op jit(solution)/shard_map/all_to_all | solution.py:536
  18.4 8.0 %fluid_kernel.1 = (f32[3,128,512]{2,1,0:T(8,128)}, f32[3,128,512]{2,1,0:T(8,128)}, f32[2,3,32,128]{3,2,1,0:T(8,128)S(1)}, f32[2,3,32,128]{3,2,1,0:T(8,128)}, f32...) custom-call(f32[3,128,512]{2,1,0:T(8,128)} %bitcast.25, f32[128,512]{1,0:T(8,128)} %bitcast.26, ...), custom_call_target="tpu_custom_call" | custom-call | tf_op jit(solution)/shard_map/fluid_kernel/pallas_call | solution.py:502
  26.4 0.7 collective-permute-start.1
  27.1 5.6 %collective-permute-start = (f32[3,32,128]{2,1,0:T(8,128)S(1)}, f32[3,32,128]{2,1,0:T(8,128)S(1)}, u32[]{:S(2)}, u32[]{:S(2)}) collective-permute-start(f32[3,32,128]{2,1,0:T(8,128)S(1)} %get-tuple-element.44), channel_id=1, source_target_pairs={{0,128},{128,0},{256,384},{384,256},{1,129},{129,1},{257,385},{385... | collective-permute-start | bytes 147464 | tf_op jit(solution)/shard_map/ppermute | solution.py:517
  32.7 5.1 %all-to-all-done.got = f32[32,13,1,128]{3,2,1,0:T(1,128)S(1)} async-done(((f32[32,13,1,128]{3,2,1,0:T(1,128)}), f32[32,13,1,128]{3,2,1,0:T(1,128)S(1)}, u32[]{:S(2)}, u32[]{:S(2)}) %all-to-all-start) | async-done | bytes 213024 | tf_op jit(solution)/shard_map/all_to_all | solution.py:536
  37.8 5.8 %fibre_kernel.1 = f32[32,12,1,128]{3,2,1,0:T(1,128)} custom-call(f32[32,13,1,128]{3,2,1,0:T(1,128)S(1)} %all-to-all-done.got, f32[6144,128]{1,0:T(8,128)S(1)} %get-tuple-element.27.table), custom_call_target="tpu_custom_call" | custom-call | tf_op jit(solution)/shard_map/fibre_kernel/pallas_call | solution.py:502
  43.6 0.0 copy-start
  43.6 0.0 copy-start.1
  43.7 0.0 collective-permute-done.1.x2_in
  43.7 0.0 copy-start.2
  43.7 0.0 collective-permute-done.x1_in
  43.7 0.0 copy-start.3
  43.7 7.0 %all-to-all-start.1 = ((f32[32,12,1,128]{3,2,1,0:T(1,128)}), f32[32,12,1,128]{3,2,1,0:T(1,128)S(1)}, u32[]{:S(2)}, u32[]{:S(2)}) async-start(f32[32,12,1,128]{3,2,1,0:T(1,128)} %fibre_kernel.1), calls=%async_computation.1 | async-start | bytes 393216 | tf_op jit(solution)/shard_map/all_to_all | solution.py:573
  50.8 0.0 copy-done.2
  50.8 0.0 copy-done.3
  50.8 1.1 %y_face_kernel.1 = (f32[3,32,128]{2,1,0:T(8,128)S(1)}, f32[3,32,128]{2,1,0:T(8,128)S(1)}, f32[3,32,128]{2,1,0:T(8,128)S(1)}, f32[3,32,128]{2,1,0:T(8,128)S(1)}, f32[2,3,16,128]{3,2,1,0:T(8,128)S(1)}) custom-call(f32[3,32,128]{2,1,0:T(8,128)} %copy-done.3, f32[3,32,128]{2,1,0:T(8,128)} %copy-done.2, f32[2,3,32,128]{3,2,1,0:T(8,128)} %get-tuple-element.31.y_in, ...), custom_call_target="tpu_custom_call" | custom-call | tf_op jit(solution)/shard_map/y_face_kernel/pallas_call | solution.py:502
  51.9 3.7 %collective-permute-start.2 = (f32[3,32,128]{2,1,0:T(8,128)S(1)}, f32[3,32,128]{2,1,0:T(8,128)S(1)}, u32[]{:S(2)}, u32[]{:S(2)}) collective-permute-start(f32[3,32,128]{2,1,0:T(8,128)S(1)} %get-tuple-element.35), channel_id=1, source_target_pairs={{0,32},{32,0},{64,96},{96,64},{1,33},{33,1},{65,97},{97,65},{2,34}... | collective-permute-start | bytes 147464 | tf_op jit(solution)/shard_map/ppermute | solution.py:517
  55.5 1.9 %collective-permute-start.3 = (f32[3,32,128]{2,1,0:T(8,128)S(1)}, f32[3,32,128]{2,1,0:T(8,128)S(1)}, u32[]{:S(2)}, u32[]{:S(2)}) collective-permute-start(f32[3,32,128]{2,1,0:T(8,128)S(1)} %get-tuple-element.36), channel_id=1, source_target_pairs={{32,64},{64,32},{33,65},{65,33},{34,66},{66,34},{35,67},{67,35},{3... | collective-permute-start | bytes 147464 | tf_op jit(solution)/shard_map/ppermute | solution.py:517
  57.5 0.0 collective-permute-done.2.y1
  57.5 3.2 %collective-permute-done.3.y2 = f32[3,32,128]{2,1,0:T(8,128)S(1)} collective-permute-done((f32[3,32,128]{2,1,0:T(8,128)S(1)}, f32[3,32,128]{2,1,0:T(8,128)S(1)}, u32[]{:S(2)}, u32[]{:S(2)}) %collective-permute-start.3) | collective-permute-done | bytes 49184 | tf_op jit(solution)/shard_map/ppermute | solution.py:517
  60.7 0.3 z_face_kernel.1
  60.9 3.3 %collective-permute-start.4 = (f32[3,16,128]{2,1,0:T(8,128)S(1)}, f32[3,16,128]{2,1,0:T(8,128)S(1)}, u32[]{:S(2)}, u32[]{:S(2)}) collective-permute-start(f32[3,16,128]{2,1,0:T(8,128)S(1)} %get-tuple-element.38), channel_id=1, source_target_pairs={{0,1},{1,0},{2,3},{3,2},{4,5},{5,4},{6,7},{7,6},{8,9},{9,8},{10,11... | collective-permute-start | bytes 73736 | tf_op jit(solution)/shard_map/ppermute | solution.py:517
  64.2 3.3 %collective-permute-start.5 = (f32[3,16,128]{2,1,0:T(8,128)S(1)}, f32[3,16,128]{2,1,0:T(8,128)S(1)}, u32[]{:S(2)}, u32[]{:S(2)}) collective-permute-start(f32[3,16,128]{2,1,0:T(8,128)S(1)} %get-tuple-element.39), channel_id=1, source_target_pairs={{1,2},{2,1},{3,4},{4,3},{5,6},{6,5},{7,8},{8,7},{9,10},{10,9},{11,... | collective-permute-start | bytes 73736 | tf_op jit(solution)/shard_map/ppermute | solution.py:517
  67.5 1.9 %side_kernel.1.work = f32[6,128,512]{2,1,0:T(8,128)S(1)} custom-call(f32[3,128,512]{2,1,0:T(8,128)} %get-tuple-element.23.adv_in, f32[3,128,512]{2,1,0:T(8,128)} %get-tuple-element.24.helm_in, f32[3,32,128]{2,1,0:T(8,128)S(1)} %get-tuple-element.33.x1, f32[3,32,128]{2,1,0:T(8,128)S(1)} %get-tuple-element.34.x2, f32[3,32,128]{2,1,0:T(8,128)S(1)} %collective-permute-done.2.y1, ...), custom_call_target="tpu_custom_call" | custom-call | tf_op jit(solution)/shard_map/side_kernel/pallas_call | solution.py:502
  69.4 0.0 collective-permute-done.4.z1
  69.4 0.2 collective-permute-done.5.z2
  69.6 1.7 %end_kernel.1 = (f32[3,128,512]{2,1,0:T(8,128)}, f32[3,128,512]{2,1,0:T(8,128)}) custom-call(f32[6,128,512]{2,1,0:T(8,128)S(1)} %side_kernel.1.work, f32[3,16,128]{2,1,0:T(8,128)S(1)} %collective-permute-done.4.z1, f32[3,16,128]{2,1,0:T(8,128)S(1)} %collective-permute-done.5.z2), custom_call_target="tpu_custom_call" | custom-call | tf_op jit(solution)/shard_map/end_kernel/pallas_call | solution.py:502
  71.3 0.0 all-to-all-done.1.sampled
  71.3 0.0 copy-done
  71.3 0.0 copy-done.1
  71.4 1.4 %drag_kernel.1 = f32[32,3,4,128]{3,2,1,0:T(4,128)} custom-call(s32[32]{0:T(128)S(1)} %bitcast.24, f32[32,12,1,128]{3,2,1,0:T(1,128)S(1)} %all-to-all-done.1.sampled, f32[32,3,4,128]{3,2,1,0:T(4,128)S(1)} %bitcast.22), custom_call_target="tpu_custom_call" | custom-call | tf_op jit(solution)/shard_map/drag_kernel/pallas_call | solution.py:502
  (1 shorter events, 0.0 us)
Async XLA Ops:
  2.4 35.4 %all-to-all-start = ((f32[32,13,1,128]{3,2,1,0:T(1,128)}), f32[32,13,1,128]{3,2,1,0:T(1,128)S(1)}, u32[]{:S(2)}, u32[]{:S(2)}) async-start(f32[32,13,1,128]{3,2,1,0:T(1,128)} %pack_kernel.1), calls=%async_computation | async-start | bytes 425984 | tf_op jit(solution)/shard_map/all_to_all | solution.py:536
  26.4 17.2 %collective-permute-start.1 = (f32[3,32,128]{2,1,0:T(8,128)S(1)}, f32[3,32,128]{2,1,0:T(8,128)S(1)}, u32[]{:S(2)}, u32[]{:S(2)}) collective-permute-start(f32[3,32,128]{2,1,0:T(8,128)S(1)} %get-tuple-element.43), channel_id=1, source_target_pairs={{128,256},{256,128},{129,257},{257,129},{130,258},{258,130},{131,2... | collective-permute-start | bytes 147464 | tf_op jit(solution)/shard_map/ppermute | solution.py:517
  27.1 16.6 %collective-permute-start = (f32[3,32,128]{2,1,0:T(8,128)S(1)}, f32[3,32,128]{2,1,0:T(8,128)S(1)}, u32[]{:S(2)}, u32[]{:S(2)}) collective-permute-start(f32[3,32,128]{2,1,0:T(8,128)S(1)} %get-tuple-element.44), channel_id=1, source_target_pairs={{0,128},{128,0},{256,384},{384,256},{1,129},{129,1},{257,385},{385... | collective-permute-start | bytes 147464 | tf_op jit(solution)/shard_map/ppermute | solution.py:517
  43.6 27.7 %copy-start = (f32[1,1,1,32,4,3,128]{6,4,5,3,2,1,0:T(4,128)S(1)}, f32[1,1,1,32,4,3,128]{6,4,5,3,2,1,0:T(4,128)}, u32[]{:S(2)}) copy-start(f32[1,1,1,32,4,3,128]{6,4,5,3,2,1,0:T(4,128)} %param.12) | copy-start | bytes 589828
  43.6 27.7 %copy-start.1 = (s32[1,1,1,32]{3,2,1,0:T(1,128)S(1)}, s32[1,1,1,32]{3,2,1,0:T(1,128)}, u32[]{:S(2)}) copy-start(s32[1,1,1,32]{3,2,1,0:T(1,128)} %param.11) | copy-start | bytes 388
  43.7 7.1 %copy-start.2 = (f32[3,32,128]{2,1,0:T(8,128)}, f32[3,32,128]{2,1,0:T(8,128)S(1)}, u32[]{:S(2)}) copy-start(f32[3,32,128]{2,1,0:T(8,128)S(1)} %collective-permute-done.1.x2_in) | copy-start | bytes 147460
  43.7 7.1 %copy-start.3 = (f32[3,32,128]{2,1,0:T(8,128)}, f32[3,32,128]{2,1,0:T(8,128)S(1)}, u32[]{:S(2)}) copy-start(f32[3,32,128]{2,1,0:T(8,128)S(1)} %collective-permute-done.x1_in) | copy-start | bytes 147460
  43.7 27.6 %all-to-all-start.1 = ((f32[32,12,1,128]{3,2,1,0:T(1,128)}), f32[32,12,1,128]{3,2,1,0:T(1,128)S(1)}, u32[]{:S(2)}, u32[]{:S(2)}) async-start(f32[32,12,1,128]{3,2,1,0:T(1,128)} %fibre_kernel.1), calls=%async_computation.1 | async-start | bytes 393216 | tf_op jit(solution)/shard_map/all_to_all | solution.py:573
  51.9 5.6 %collective-permute-start.2 = (f32[3,32,128]{2,1,0:T(8,128)S(1)}, f32[3,32,128]{2,1,0:T(8,128)S(1)}, u32[]{:S(2)}, u32[]{:S(2)}) collective-permute-start(f32[3,32,128]{2,1,0:T(8,128)S(1)} %get-tuple-element.35), channel_id=1, source_target_pairs={{0,32},{32,0},{64,96},{96,64},{1,33},{33,1},{65,97},{97,65},{2,34}... | collective-permute-start | bytes 147464 | tf_op jit(solution)/shard_map/ppermute | solution.py:517
  55.5 5.1 %collective-permute-start.3 = (f32[3,32,128]{2,1,0:T(8,128)S(1)}, f32[3,32,128]{2,1,0:T(8,128)S(1)}, u32[]{:S(2)}, u32[]{:S(2)}) collective-permute-start(f32[3,32,128]{2,1,0:T(8,128)S(1)} %get-tuple-element.36), channel_id=1, source_target_pairs={{32,64},{64,32},{33,65},{65,33},{34,66},{66,34},{35,67},{67,35},{3... | collective-permute-start | bytes 147464 | tf_op jit(solution)/shard_map/ppermute | solution.py:517
  60.9 8.5 %collective-permute-start.4 = (f32[3,16,128]{2,1,0:T(8,128)S(1)}, f32[3,16,128]{2,1,0:T(8,128)S(1)}, u32[]{:S(2)}, u32[]{:S(2)}) collective-permute-start(f32[3,16,128]{2,1,0:T(8,128)S(1)} %get-tuple-element.38), channel_id=1, source_target_pairs={{0,1},{1,0},{2,3},{3,2},{4,5},{5,4},{6,7},{7,6},{8,9},{9,8},{10,11... | collective-permute-start | bytes 73736 | tf_op jit(solution)/shard_map/ppermute | solution.py:517
  64.2 5.4 %collective-permute-start.5 = (f32[3,16,128]{2,1,0:T(8,128)S(1)}, f32[3,16,128]{2,1,0:T(8,128)S(1)}, u32[]{:S(2)}, u32[]{:S(2)}) collective-permute-start(f32[3,16,128]{2,1,0:T(8,128)S(1)} %get-tuple-element.39), channel_id=1, source_target_pairs={{1,2},{2,1},{3,4},{4,3},{5,6},{6,5},{7,8},{8,7},{9,10},{10,9},{11,... | collective-permute-start | bytes 73736 | tf_op jit(solution)/shard_map/ppermute | solution.py:517

commit v4 on v3

--- a/solution.py
+++ b/solution.py
@@ -28,7 +28,7 @@
 )
 helm_shift = 20.0
 drag_scale = 0.5
-UNROLL = 8
+UNROLL = 16
 VMEM_LIMIT = 48 * 1024 * 1024
 f32 = jnp.float32
 bf16 = jnp.bfloat16
@@ -150,6 +150,14 @@
 def pick(x, table):
     high, low = split(x)
     return mm(high, table) + mm(low, table)
+
+
+def pick_both(first, second, table):
+    rows = first.shape[0]
+    got = mm(jnp.concatenate(split(first) + split(second), 0), table)
+    one = got[0:rows] + got[rows : 2 * rows]
+    two = got[2 * rows : 3 * rows] + got[3 * rows :]
+    return one + pltpu.roll(two, 64, 1)
 
 
 def spread(x, table):
@@ -206,17 +214,11 @@
         x_work[1 - odd, c] = left
         x_work[odd, c] = right
     for out, start, side in ((y_work.at[0], 0, 0), (y_work.at[1], 24, 1)):
-        faces = []
-        for field in (adv, helm):
-            rows = field[...].reshape(12, 32, 512)[:, start : start + 8].reshape(96, 512)
-            faces.append(pick(rows, pick_table(side)))
-        out[...] = (faces[0] + pltpu.roll(faces[1], 64, 1)).reshape(3, 32, 128)
+        faces = [field[...].reshape(12, 32, 512)[:, start : start + 8].reshape(96, 512) for field in (adv, helm)]
+        out[...] = pick_both(*faces, pick_table(side)).reshape(3, 32, 128)
     for out, start, side in ((z_work.at[0], 0, 2), (z_work.at[1], 7, 3)):
-        faces = []
-        for field in (adv, helm):
-            rows = field[...].reshape(48, 8, 512)[:, start]
-            faces.append(pick(rows, pick_table(side)))
-        out[...] = (faces[0] + pltpu.roll(faces[1], 64, 1)).reshape(3, 16, 128)
+        faces = [field[...].reshape(48, 8, 512)[:, start] for field in (adv, helm)]
+        out[...] = pick_both(*faces, pick_table(side)).reshape(3, 16, 128)
     stores.append(pltpu.make_async_copy(y_work, y_out, sems.at[12]))
     stores[-1].start()
     stores.append(pltpu.make_async_copy(z_work, z_out, sems.at[13]))
@@ -387,20 +389,31 @@
             out[source, d] = jnp.where(slot < counts[source], factor * relative[d], 0.0)
 
 
-def pack_kernel(coords_in, idents_in, counts_in, out, coords, idents, counts, sems):
-    pairs = ((coords_in, coords), (idents_in, idents), (counts_in, counts))
+def pack_kernel(coords_in, idents_in, counts_in, out_hbm, coords, idents, counts, out, sems):
+    pairs = [(idents_in, idents), (counts_in, counts)]
+    for part in range(4):
+        rows = pl.ds(8 * part, 8)
+        pairs.append((coords_in.at[rows], coords.at[rows]))
     loads = [pltpu.make_async_copy(a, b, sems.at[n]) for n, (a, b) in enumerate(pairs)]
     for load in loads:
         load.start()
-    for load in loads:
-        load.wait()
+    loads[0].wait()
+    loads[1].wait()
     slot = lax.broadcasted_iota(jnp.int32, (4, 32), 0)
     tags = jnp.where(slot < counts[...], idents[...], -1).astype(f32)
     tags = jnp.concatenate([tags[q : q + 1] for q in range(4)], axis=1)
-    for source in range(32):
-        for d in range(3):
-            out[source, 4 * d : 4 * d + 4, 0] = coords[source, d]
-        out[source, 12] = tags
+    stores = []
+    for part in range(4):
+        loads[2 + part].wait()
+        for source in range(8 * part, 8 * part + 8):
+            for d in range(3):
+                out[source, 4 * d : 4 * d + 4, 0] = coords[source, d]
+            out[source, 12] = tags
+        rows = pl.ds(8 * part, 8)
+        stores.append(pltpu.make_async_copy(out.at[rows], out_hbm.at[rows], sems.at[6 + part]))
+        stores[-1].start()
+    for store in stores:
+        store.wait()
 
 
 def fill_table(vel, table, tiles):
@@ -458,13 +471,16 @@
         high = basis_z.astype(bf16).astype(f32)
         low = basis_z - high
         zero = jnp.zeros((8, 128), f32)
+        empty = jnp.zeros((16, 128), bf16)
+        highs = [jnp.concatenate(pair, 0).astype(bf16) for pair in ((high, zero), (zero, high))]
+        lows = [jnp.concatenate(pair, 0).astype(bf16) for pair in ((low, zero), (zero, low))]
         columns = []
         for j in range(4):
-            pieces = [zero] * 16
-            pieces[j] = high
-            pieces[4 + j] = high
-            pieces[8 + j] = low
-            columns.append(jnp.concatenate(pieces, 0).astype(bf16))
+            pieces = [empty] * 8
+            pieces[j // 2] = highs[j % 2]
+            pieces[2 + j // 2] = highs[j % 2]
+            pieces[4 + j // 2] = lows[j % 2]
+            columns.append(jnp.concatenate(pieces, 0))
         sections = [mm(nodes, column) for column in columns]
         for c in range(3):
             total = jnp.zeros((8, 128), f32)
@@ -525,12 +541,13 @@
     counts = block_count.reshape(32)
     own_velocity = fibre_velocity.reshape(32, 4, 3, 128).transpose(0, 2, 1, 3)
     (packed,) = call(
-        pack_kernel, [(32, 13, 1, 128)], (coords, idents, counts.reshape(1, 32)), specs=[hbm] * 3,
+        pack_kernel, [(32, 13, 1, 128)], (coords, idents, counts.reshape(1, 32)), specs=[hbm] * 3, out_specs=[hbm],
         scratch=[
             pltpu.VMEM((32, 3, 4, 128), f32),
             pltpu.VMEM((4, 32), jnp.int32),
             pltpu.VMEM((1, 32), jnp.int32),
-            pltpu.SemaphoreType.DMA((3,)),
+            pltpu.VMEM((32, 13, 1, 128), f32),
+            pltpu.SemaphoreType.DMA((10,)),
         ],
     )
     got = lax.all_to_all(packed, "gz", split_axis=0, concat_axis=0, tiled=True)

time: 73.3 us -> 72.2 us (0.985)
  Pallas kernels: 22 us -> 20.5 us
    pallas_call x8, Pallas kernels: 22 us -> 20.5 us  [call(): pl.pallas_call(kernel, out_shape=shapes, in_specs=specs or [vmem] * len(a...]
  transfers between devices with their start and end apart: 8 -> 8, of which waited for: 3 -> 3; matrix products, arithmetic and copies ran while one was open for 0% -> 0% of each run, Pallas kernels for 26% -> 24%
where the time goes in v4:
time: 72.2 us; the launch traced here: 71.8 us
  starting transfers between devices  41.8 us (58%)
  Pallas kernels  20.5 us (28%)
  waiting for transfers between devices  8.69 us (12%)
  between operations  0.86 us (1%)
    pallas_call x8, Pallas kernels, call(): pl.pallas_call(kernel, out_shape=shapes, in_specs=specs or [vmem] * len(a...  20.5 us
    all_to_all x1, starting transfers between devices, body(): got = lax.all_to_all(packed, 'gz', split_axis=0, concat_axis=0, tiled=True)  15.9 us
    ppermute x3, starting transfers between devices, swap(): lax.ppermute(first, axis, even_pairs)  12.3 us
    all_to_all x1, starting transfers between devices, body(): lax.all_to_all(values, 'gz', split_axis=0, concat_axis=0, tiled=True)  7.62 us
    ppermute x3, starting transfers between devices, swap(): lax.ppermute(second, axis, odd_pairs)  5.9 us
    all_to_all x1, waiting for transfers between devices, body(): got = lax.all_to_all(packed, 'gz', split_axis=0, concat_axis=0, tiled=True)  5.28 us
    ppermute x3, waiting for transfers between devices, swap(): lax.ppermute(second, axis, odd_pairs)  3.4 us
  transfers between devices with their start and end apart: 8, of which 3 were waited for; matrix products, arithmetic and copies ran while one was open for 0% of the time, Pallas kernels for 24%

profile of v4, /device:TPU:17, one launch (start us, length us, event | category | flops | bytes accessed | tf_op | source)
XLA Modules:
  0.0 71.8 jit_solution(4779273287937977819)
XLA Ops:
  0.6 1.7 %pack_kernel.1 = f32[32,13,1,128]{3,2,1,0:T(1,128)} custom-call(f32[32,3,4,128]{3,2,1,0:T(4,128)} %bitcast.27, s32[4,32]{1,0:T(4,128)} %bitcast.29, s32[1,32]{1,0:T(1,128)} %bitcast.23), custom_call_target="tpu_custom_call" | custom-call | tf_op jit(solution)/shard_map/pack_kernel/pallas_call | solution.py:518
  2.3 15.9 %all-to-all-start = ((f32[32,13,1,128]{3,2,1,0:T(1,128)}), f32[32,13,1,128]{3,2,1,0:T(1,128)S(1)}, u32[]{:S(2)}, u32[]{:S(2)}) async-start(f32[32,13,1,128]{3,2,1,0:T(1,128)} %pack_kernel.1), calls=%async_computation | async-start | bytes 425984 | tf_op jit(solution)/shard_map/all_to_all | solution.py:553
  18.3 7.9 %fluid_kernel.1 = (f32[3,128,512]{2,1,0:T(8,128)}, f32[3,128,512]{2,1,0:T(8,128)}, f32[2,3,32,128]{3,2,1,0:T(8,128)S(1)}, f32[2,3,32,128]{3,2,1,0:T(8,128)}, f32...) custom-call(f32[3,128,512]{2,1,0:T(8,128)} %bitcast.25, f32[128,512]{1,0:T(8,128)} %bitcast.26, ...), custom_call_target="tpu_custom_call" | custom-call | tf_op jit(solution)/shard_map/fluid_kernel/pallas_call | solution.py:518
  26.2 0.7 collective-permute-start.1
  26.8 5.6 %collective-permute-start = (f32[3,32,128]{2,1,0:T(8,128)S(1)}, f32[3,32,128]{2,1,0:T(8,128)S(1)}, u32[]{:S(2)}, u32[]{:S(2)}) collective-permute-start(f32[3,32,128]{2,1,0:T(8,128)S(1)} %get-tuple-element.44), channel_id=1, source_target_pairs={{0,128},{128,0},{256,384},{384,256},{1,129},{129,1},{257,385},{385... | collective-permute-start | bytes 147464 | tf_op jit(solution)/shard_map/ppermute | solution.py:533
  32.4 5.3 %all-to-all-done.got = f32[32,13,1,128]{3,2,1,0:T(1,128)S(1)} async-done(((f32[32,13,1,128]{3,2,1,0:T(1,128)}), f32[32,13,1,128]{3,2,1,0:T(1,128)S(1)}, u32[]{:S(2)}, u32[]{:S(2)}) %all-to-all-start) | async-done | bytes 213024 | tf_op jit(solution)/shard_map/all_to_all | solution.py:553
  37.7 4.6 %fibre_kernel.1 = f32[32,12,1,128]{3,2,1,0:T(1,128)} custom-call(f32[32,13,1,128]{3,2,1,0:T(1,128)S(1)} %all-to-all-done.got, f32[6144,128]{1,0:T(8,128)S(1)} %get-tuple-element.27.table), custom_call_target="tpu_custom_call" | custom-call | tf_op jit(solution)/shard_map/fibre_kernel/pallas_call | solution.py:518
  42.3 0.0 copy-start
  42.3 0.0 copy-start.1
  42.3 0.0 collective-permute-done.1.x2_in
  42.3 0.0 copy-start.2
  42.3 0.0 collective-permute-done.x1_in
  42.3 0.0 copy-start.3
  42.3 7.6 %all-to-all-start.1 = ((f32[32,12,1,128]{3,2,1,0:T(1,128)}), f32[32,12,1,128]{3,2,1,0:T(1,128)S(1)}, u32[]{:S(2)}, u32[]{:S(2)}) async-start(f32[32,12,1,128]{3,2,1,0:T(1,128)} %fibre_kernel.1), calls=%async_computation.1 | async-start | bytes 393216 | tf_op jit(solution)/shard_map/all_to_all | solution.py:590
  50.0 0.0 copy-done.2
  50.0 0.0 copy-done.3
  50.0 1.1 %y_face_kernel.1 = (f32[3,32,128]{2,1,0:T(8,128)S(1)}, f32[3,32,128]{2,1,0:T(8,128)S(1)}, f32[3,32,128]{2,1,0:T(8,128)S(1)}, f32[3,32,128]{2,1,0:T(8,128)S(1)}, f32[2,3,16,128]{3,2,1,0:T(8,128)S(1)}) custom-call(f32[3,32,128]{2,1,0:T(8,128)} %copy-done.3, f32[3,32,128]{2,1,0:T(8,128)} %copy-done.2, f32[2,3,32,128]{3,2,1,0:T(8,128)} %get-tuple-element.31.y_in, ...), custom_call_target="tpu_custom_call" | custom-call | tf_op jit(solution)/shard_map/y_face_kernel/pallas_call | solution.py:518
  51.1 3.5 %collective-permute-start.2 = (f32[3,32,128]{2,1,0:T(8,128)S(1)}, f32[3,32,128]{2,1,0:T(8,128)S(1)}, u32[]{:S(2)}, u32[]{:S(2)}) collective-permute-start(f32[3,32,128]{2,1,0:T(8,128)S(1)} %get-tuple-element.35), channel_id=1, source_target_pairs={{0,32},{32,0},{64,96},{96,64},{1,33},{33,1},{65,97},{97,65},{2,34}... | collective-permute-start | bytes 147464 | tf_op jit(solution)/shard_map/ppermute | solution.py:533
  54.6 1.9 %collective-permute-start.3 = (f32[3,32,128]{2,1,0:T(8,128)S(1)}, f32[3,32,128]{2,1,0:T(8,128)S(1)}, u32[]{:S(2)}, u32[]{:S(2)}) collective-permute-start(f32[3,32,128]{2,1,0:T(8,128)S(1)} %get-tuple-element.36), channel_id=1, source_target_pairs={{32,64},{64,32},{33,65},{65,33},{34,66},{66,34},{35,67},{67,35},{3... | collective-permute-start | bytes 147464 | tf_op jit(solution)/shard_map/ppermute | solution.py:533
  56.5 0.0 collective-permute-done.2.y1
  56.5 3.2 %collective-permute-done.3.y2 = f32[3,32,128]{2,1,0:T(8,128)S(1)} collective-permute-done((f32[3,32,128]{2,1,0:T(8,128)S(1)}, f32[3,32,128]{2,1,0:T(8,128)S(1)}, u32[]{:S(2)}, u32[]{:S(2)}) %collective-permute-start.3) | collective-permute-done | bytes 49184 | tf_op jit(solution)/shard_map/ppermute | solution.py:533
  59.7 0.3 z_face_kernel.1
  60.0 3.3 %collective-permute-start.4 = (f32[3,16,128]{2,1,0:T(8,128)S(1)}, f32[3,16,128]{2,1,0:T(8,128)S(1)}, u32[]{:S(2)}, u32[]{:S(2)}) collective-permute-start(f32[3,16,128]{2,1,0:T(8,128)S(1)} %get-tuple-element.38), channel_id=1, source_target_pairs={{0,1},{1,0},{2,3},{3,2},{4,5},{5,4},{6,7},{7,6},{8,9},{9,8},{10,11... | collective-permute-start | bytes 73736 | tf_op jit(solution)/shard_map/ppermute | solution.py:533
  63.2 3.3 %collective-permute-start.5 = (f32[3,16,128]{2,1,0:T(8,128)S(1)}, f32[3,16,128]{2,1,0:T(8,128)S(1)}, u32[]{:S(2)}, u32[]{:S(2)}) collective-permute-start(f32[3,16,128]{2,1,0:T(8,128)S(1)} %get-tuple-element.39), channel_id=1, source_target_pairs={{1,2},{2,1},{3,4},{4,3},{5,6},{6,5},{7,8},{8,7},{9,10},{10,9},{11,... | collective-permute-start | bytes 73736 | tf_op jit(solution)/shard_map/ppermute | solution.py:533
  66.6 1.9 %side_kernel.1.work = f32[6,128,512]{2,1,0:T(8,128)S(1)} custom-call(f32[3,128,512]{2,1,0:T(8,128)} %get-tuple-element.23.adv_in, f32[3,128,512]{2,1,0:T(8,128)} %get-tuple-element.24.helm_in, f32[3,32,128]{2,1,0:T(8,128)S(1)} %get-tuple-element.33.x1, f32[3,32,128]{2,1,0:T(8,128)S(1)} %get-tuple-element.34.x2, f32[3,32,128]{2,1,0:T(8,128)S(1)} %collective-permute-done.2.y1, ...), custom_call_target="tpu_custom_call" | custom-call | tf_op jit(solution)/shard_map/side_kernel/pallas_call | solution.py:518
  68.5 0.0 collective-permute-done.4.z1
  68.5 0.2 collective-permute-done.5.z2
  68.7 1.7 %end_kernel.1 = (f32[3,128,512]{2,1,0:T(8,128)}, f32[3,128,512]{2,1,0:T(8,128)}) custom-call(f32[6,128,512]{2,1,0:T(8,128)S(1)} %side_kernel.1.work, f32[3,16,128]{2,1,0:T(8,128)S(1)} %collective-permute-done.4.z1, f32[3,16,128]{2,1,0:T(8,128)S(1)} %collective-permute-done.5.z2), custom_call_target="tpu_custom_call" | custom-call | tf_op jit(solution)/shard_map/end_kernel/pallas_call | solution.py:518
  70.4 0.0 all-to-all-done.1.sampled
  70.4 0.0 copy-done
  70.4 0.0 copy-done.1
  70.4 1.4 %drag_kernel.1 = f32[32,3,4,128]{3,2,1,0:T(4,128)} custom-call(s32[32]{0:T(128)S(1)} %bitcast.24, f32[32,12,1,128]{3,2,1,0:T(1,128)S(1)} %all-to-all-done.1.sampled, f32[32,3,4,128]{3,2,1,0:T(4,128)S(1)} %bitcast.22), custom_call_target="tpu_custom_call" | custom-call | tf_op jit(solution)/shard_map/drag_kernel/pallas_call | solution.py:518
  (1 shorter events, 0.0 us)
Async XLA Ops:
  2.3 35.4 %all-to-all-start = ((f32[32,13,1,128]{3,2,1,0:T(1,128)}), f32[32,13,1,128]{3,2,1,0:T(1,128)S(1)}, u32[]{:S(2)}, u32[]{:S(2)}) async-start(f32[32,13,1,128]{3,2,1,0:T(1,128)} %pack_kernel.1), calls=%async_computation | async-start | bytes 425984 | tf_op jit(solution)/shard_map/all_to_all | solution.py:553
  26.2 16.1 %collective-permute-start.1 = (f32[3,32,128]{2,1,0:T(8,128)S(1)}, f32[3,32,128]{2,1,0:T(8,128)S(1)}, u32[]{:S(2)}, u32[]{:S(2)}) collective-permute-start(f32[3,32,128]{2,1,0:T(8,128)S(1)} %get-tuple-element.43), channel_id=1, source_target_pairs={{128,256},{256,128},{129,257},{257,129},{130,258},{258,130},{131,2... | collective-permute-start | bytes 147464 | tf_op jit(solution)/shard_map/ppermute | solution.py:533
  26.8 15.5 %collective-permute-start = (f32[3,32,128]{2,1,0:T(8,128)S(1)}, f32[3,32,128]{2,1,0:T(8,128)S(1)}, u32[]{:S(2)}, u32[]{:S(2)}) collective-permute-start(f32[3,32,128]{2,1,0:T(8,128)S(1)} %get-tuple-element.44), channel_id=1, source_target_pairs={{0,128},{128,0},{256,384},{384,256},{1,129},{129,1},{257,385},{385... | collective-permute-start | bytes 147464 | tf_op jit(solution)/shard_map/ppermute | solution.py:533
  42.3 28.1 %copy-start = (f32[1,1,1,32,4,3,128]{6,4,5,3,2,1,0:T(4,128)S(1)}, f32[1,1,1,32,4,3,128]{6,4,5,3,2,1,0:T(4,128)}, u32[]{:S(2)}) copy-start(f32[1,1,1,32,4,3,128]{6,4,5,3,2,1,0:T(4,128)} %param.12) | copy-start | bytes 589828
  42.3 28.1 %copy-start.1 = (s32[1,1,1,32]{3,2,1,0:T(1,128)S(1)}, s32[1,1,1,32]{3,2,1,0:T(1,128)}, u32[]{:S(2)}) copy-start(s32[1,1,1,32]{3,2,1,0:T(1,128)} %param.11) | copy-start | bytes 388
  42.3 7.7 %copy-start.2 = (f32[3,32,128]{2,1,0:T(8,128)}, f32[3,32,128]{2,1,0:T(8,128)S(1)}, u32[]{:S(2)}) copy-start(f32[3,32,128]{2,1,0:T(8,128)S(1)} %collective-permute-done.1.x2_in) | copy-start | bytes 147460
  42.3 7.6 %copy-start.3 = (f32[3,32,128]{2,1,0:T(8,128)}, f32[3,32,128]{2,1,0:T(8,128)S(1)}, u32[]{:S(2)}) copy-start(f32[3,32,128]{2,1,0:T(8,128)S(1)} %collective-permute-done.x1_in) | copy-start | bytes 147460
  42.3 28.0 %all-to-all-start.1 = ((f32[32,12,1,128]{3,2,1,0:T(1,128)}), f32[32,12,1,128]{3,2,1,0:T(1,128)S(1)}, u32[]{:S(2)}, u32[]{:S(2)}) async-start(f32[32,12,1,128]{3,2,1,0:T(1,128)} %fibre_kernel.1), calls=%async_computation.1 | async-start | bytes 393216 | tf_op jit(solution)/shard_map/all_to_all | solution.py:590
  51.1 5.4 %collective-permute-start.2 = (f32[3,32,128]{2,1,0:T(8,128)S(1)}, f32[3,32,128]{2,1,0:T(8,128)S(1)}, u32[]{:S(2)}, u32[]{:S(2)}) collective-permute-start(f32[3,32,128]{2,1,0:T(8,128)S(1)} %get-tuple-element.35), channel_id=1, source_target_pairs={{0,32},{32,0},{64,96},{96,64},{1,33},{33,1},{65,97},{97,65},{2,34}... | collective-permute-start | bytes 147464 | tf_op jit(solution)/shard_map/ppermute | solution.py:533
  54.6 5.1 %collective-permute-start.3 = (f32[3,32,128]{2,1,0:T(8,128)S(1)}, f32[3,32,128]{2,1,0:T(8,128)S(1)}, u32[]{:S(2)}, u32[]{:S(2)}) collective-permute-start(f32[3,32,128]{2,1,0:T(8,128)S(1)} %get-tuple-element.36), channel_id=1, source_target_pairs={{32,64},{64,32},{33,65},{65,33},{34,66},{66,34},{35,67},{67,35},{3... | collective-permute-start | bytes 147464 | tf_op jit(solution)/shard_map/ppermute | solution.py:533
  60.0 8.5 %collective-permute-start.4 = (f32[3,16,128]{2,1,0:T(8,128)S(1)}, f32[3,16,128]{2,1,0:T(8,128)S(1)}, u32[]{:S(2)}, u32[]{:S(2)}) collective-permute-start(f32[3,16,128]{2,1,0:T(8,128)S(1)} %get-tuple-element.38), channel_id=1, source_target_pairs={{0,1},{1,0},{2,3},{3,2},{4,5},{5,4},{6,7},{7,6},{8,9},{9,8},{10,11... | collective-permute-start | bytes 73736 | tf_op jit(solution)/shard_map/ppermute | solution.py:533
  63.2 5.4 %collective-permute-start.5 = (f32[3,16,128]{2,1,0:T(8,128)S(1)}, f32[3,16,128]{2,1,0:T(8,128)S(1)}, u32[]{:S(2)}, u32[]{:S(2)}) collective-permute-start(f32[3,16,128]{2,1,0:T(8,128)S(1)} %get-tuple-element.39), channel_id=1, source_target_pairs={{1,2},{2,1},{3,4},{4,3},{5,6},{6,5},{7,8},{8,7},{9,10},{10,9},{11,... | collective-permute-start | bytes 73736 | tf_op jit(solution)/shard_map/ppermute | solution.py:533
